TPU v7x, 32 devices: a whole 2x2x4 slice. The times are simulated.
32 devices in a mesh: grp: 2 (over x), chan: 16 (over z, y, core).
Axes of the slice: x: 2, y: 2, z: 4, core: 2. Of those that a mesh axis runs over, the one named last changes fastest.
Arguments:
- voltages: bfloat16 [8192, 2, 64, 128], P(('grp', 'chan')), parts along dimension 0, may hold values from -9 to 9
- delays: float32 [512, 64], replicated, may hold values from -2 to 2
- pointing: int32 [32], P('grp'), parts along dimension 0, may hold values from 0 to 511
- dm_index: int32 [32], P(('grp', 'chan')), parts along dimension 0, may hold values from 0 to 511
- dish_mask: int32 [128], P('grp'), parts along dimension 0, may hold values 0 or 1
Outputs:
- dedispersed: float32 [32, 2, 128, 4096], P(('grp', 'chan')), parts along dimension 0
There are 2 independent parts, one for each index of `grp`. A program takes and returns all parts, laid end to end along the dimension named above; an argument that names none is the same for every part. Nothing has to cross between parts.
All inputs are finite; a program needn't handle non-finite values.
Results may differ from a plain program's by a relative error of at most 0.005.
Values may be sent and summed in bfloat16 or wider, within the bound.
No kernel may reach another device: no remote copies, remote signals or barrier semaphores. Data moves between devices by JAX's collectives and lax.ppermute only.
A program may use at most 64 MiB of HBM per device.

v0:
```python
import functools
import math

import jax
import jax.numpy as jnp
from jax import lax
from jax.experimental import pallas as pl
from jax.experimental.pallas import tpu as pltpu
from jax.sharding import PartitionSpec as P

TWO_PI = 2.0 * math.pi
BAND_LOW = 0.856
BAND_WIDTH = 0.856
EPSILON = 1e-06
F32 = jnp.float32
BF16 = jnp.bfloat16


def cmul(a, b):
    return (a[0] * b[0] - a[1] * b[1], a[0] * b[1] + a[1] * b[0])


def cadd(a, b):
    return (a[0] + b[0], a[1] + b[1])


def csub(a, b):
    return (a[0] - b[0], a[1] - b[1])


def turn(a, num, den):
    num = num % den
    if num == 0:
        return a
    if 2 * num == den:
        return (-a[0], -a[1])
    if 4 * num == den:
        return (-a[1], a[0])
    if 4 * num == 3 * den:
        return (a[1], -a[0])
    if 8 * num % den == 0:
        root = math.sqrt(0.5)
        plus, minus = (a[0] + a[1]) * root, (a[0] - a[1]) * root
        return {1: (minus, plus), 3: (-plus, minus), 5: (-minus, -plus), 7: (plus, -minus)}[
            8 * num // den
        ]
    cosine, sine = math.cos(TWO_PI * num / den), math.sin(TWO_PI * num / den)
    return (a[0] * cosine - a[1] * sine, a[0] * sine + a[1] * cosine)


def fft_list(values, sign):
    points = len(values)
    if points == 1:
        return values
    if points == 2:
        return [cadd(values[0], values[1]), csub(values[0], values[1])]
    quarter = points // 4
    parts = [fft_list(values[i::4], sign) for i in range(4)]
    out = [None] * points
    for k in range(quarter):
        a, b, c, d = [turn(parts[i][k], sign * i * k, points) for i in range(4)]
        s0, s1 = cadd(a, c), csub(a, c)
        s2, s3 = cadd(b, d), turn(csub(b, d), sign, 4)
        out[k] = cadd(s0, s2)
        out[k + quarter] = cadd(s1, s3)
        out[k + 2 * quarter] = csub(s0, s2)
        out[k + 3 * quarter] = csub(s1, s3)
    return out


def beam_kernel(
    chans, comb, point_ref, delay_ref, mask_ref, volt_ref, out_ref, zero_ref, fine_ref, coarse_ref, rows_ref
):
    step = pl.program_id(0)
    part_rows, combs = volt_ref.shape[0], volt_ref.shape[1]
    beams = out_ref.shape[0]
    dishes = delay_ref.shape[0]
    chan_dev = part_rows * comb

    @pl.when(step == 0)
    def _():
        table_rows = delay_ref.shape[1]
        place = lax.broadcasted_iota(jnp.int32, (beams, table_rows), 1)
        which = lax.broadcasted_iota(jnp.int32, (beams, table_rows), 0)
        wanted = jnp.zeros((beams, table_rows), jnp.int32)
        for b in range(beams):
            wanted = jnp.where(which == b, point_ref[b], wanted)
        select = (wanted == place).astype(F32)
        doubled = jnp.concatenate([delay_ref[...], delay_ref[...]], 0)
        tau = lax.dot_general(
            select,
            doubled,
            (((1,), (1,)), ((), ())),
            precision=lax.Precision.HIGHEST,
            preferred_element_type=F32,
        )
        first = lax.axis_index("chan") * chan_dev
        frequency = BAND_LOW + BAND_WIDTH * (first.astype(F32) + 0.5) / chans
        angle = (TWO_PI * frequency) * tau
        gain_half = mask_ref[...].astype(F32) / math.sqrt(dishes)
        gain = jnp.concatenate([gain_half, gain_half], 1)
        cosine, sine = jnp.cos(angle) * gain, jnp.sin(angle) * gain
        left = lax.broadcasted_iota(jnp.int32, (beams, 2 * dishes), 1) < dishes
        zero_ref[0] = jnp.where(left, cosine, sine)
        zero_ref[1] = jnp.where(left, -sine, cosine)
        for table_ref, stride in ((fine_ref, 1), (coarse_ref, comb)):
            shift = (TWO_PI * BAND_WIDTH / chans * stride) * tau
            count = table_ref.shape[0]
            powers = [(jnp.ones_like(tau), jnp.zeros_like(tau)), (jnp.cos(shift), -jnp.sin(shift))]
            for k in range(2, count):
                powers.append(cmul(powers[k // 2], powers[k - k // 2]))
            for k in range(count):
                table_ref[k, 0] = powers[k][0]
                table_ref[k, 1] = powers[k][1]

    group = rows_ref.shape[1] // beams
    for g in range(part_rows * combs // group):
        for i in range(group):
            row = g * group + i
            ja, cb = row % part_rows, row // part_rows
            base = cmul(
                (zero_ref[0], zero_ref[1]),
                (fine_ref[step * combs + cb, 0], fine_ref[step * combs + cb, 1]),
            )
            weight = cmul(base, (coarse_ref[ja, 0], coarse_ref[ja, 1]))
            stacked = jnp.concatenate(weight, 0).astype(BF16)
            formed = jnp.dot(stacked, volt_ref[ja, cb], preferred_element_type=F32)
            rows_ref[0, pl.ds(i, beams, stride=group), :] = formed[:beams]
            rows_ref[1, pl.ds(i, beams, stride=group), :] = formed[beams:]
        samples = rows_ref.shape[2]
        for p in range(2):
            out_ref[:, g * group : (g + 1) * group, p * samples : (p + 1) * samples] = (
                rows_ref[p].reshape(beams, group, samples).astype(BF16)
            )


def form_beams(voltages, delays, pointing, dish_mask, chans, comb):
    chan_dev, _, dishes, samples = voltages.shape
    beams = pointing.shape[0]
    part_rows = chan_dev // comb
    combs = max(2, 16 // part_rows)
    group = 16
    volt = voltages.reshape(part_rows, comb, 2 * dishes, samples)
    return pl.pallas_call(
        functools.partial(beam_kernel, chans, comb),
        out_shape=jax.ShapeDtypeStruct((beams, chan_dev, 2 * samples), BF16),
        grid=(comb // combs,),
        in_specs=[
            pl.BlockSpec(memory_space=pltpu.SMEM),
            pl.BlockSpec((dishes, delays.shape[0]), lambda i: (0, 0)),
            pl.BlockSpec((1, dishes), lambda i: (0, 0)),
            pl.BlockSpec((part_rows, combs, 2 * dishes, samples), lambda i: (0, i, 0, 0)),
        ],
        out_specs=pl.BlockSpec((beams, part_rows * combs, 2 * samples), lambda i: (0, i, 0)),
        scratch_shapes=[
            pltpu.VMEM((2, beams, 2 * dishes), F32),
            pltpu.VMEM((comb, 2, beams, 2 * dishes), F32),
            pltpu.VMEM((part_rows, 2, beams, 2 * dishes), F32),
            pltpu.VMEM((2, beams * group, samples), F32),
        ],
        compiler_params=pltpu.CompilerParams(vmem_limit_bytes=40 * 2**20),
        name="form_beams",
    )(pointing, delays.T, dish_mask.reshape(1, dishes), volt)


def phasor(phase, points):
    half = points // 2
    angle = (TWO_PI / points) * ((phase + half) % points - half).astype(F32)
    return jnp.stack([jnp.cos(angle), jnp.sin(angle)], 0)


def chirp_tables(rate, samples, chans):
    length = samples * chans
    low, comb = 2 * samples, chans // (2 * samples)
    f = jnp.arange(samples, dtype=jnp.int32)[None, :]
    shift = 2 * rate * f % chans
    shift_low, shift_high = shift % low, shift // low
    inverse = rate * (2 - rate * rate) % (2 * comb)
    m = jnp.arange(comb, dtype=jnp.int32)[:, None]
    unit = length // (2 * comb)
    c_a = jnp.arange(samples, dtype=jnp.int32)[:, None]
    turn_a = phasor(-(rate * c_a * f % samples), samples)
    turn_b = phasor(-(rate * m * f % (chans // 2)), chans // 2)
    quad = inverse * m * m % (2 * comb) * unit
    before = [phasor(quad - (m - shift_high - beta) % comb * low * f, length) for beta in range(2)]
    place = rate * m % comb
    quad = inverse * place * place % (2 * comb) * unit
    gauss_phase = -(rate * m * m % (2 * comb)) * unit
    gauss = jnp.sum(phasor(gauss_phase, length), axis=1)
    scale = 2 * samples / (length * math.sqrt(chans))
    after = []
    for beta in range(2):
        turned = phasor(
            quad + low * place * f + f * (shift_low - low * beta) - rate * f * f % length, length
        )
        real, imag = cmul((turned[0], turned[1]), (gauss[0] * scale, gauss[1] * scale))
        after.append(jnp.stack([real, imag], 0))
    return turn_a, turn_b, jnp.stack(before), jnp.stack(after), shift_low


def transforms(samples, chans):
    low, comb = 2 * samples, chans // (2 * samples)
    t = jnp.arange(samples, dtype=jnp.int32)
    cosine, sine = phasor(t[:, None] * t[None, :] % samples, samples)
    time_mat = jnp.concatenate(
        [jnp.concatenate([cosine, -sine], 1), jnp.concatenate([sine, cosine], 1)], 0
    )
    n = jnp.arange(low, dtype=jnp.int32)
    c_b = jnp.arange(comb, dtype=jnp.int32)
    product = (comb * n[None, None, :] + c_b[:, None, None]) * n[None, :, None] % chans
    cosine, sine = phasor(product, chans)
    return time_mat.astype(BF16), jnp.concatenate([cosine, sine], 1).astype(BF16)


def dedisperse_kernel(
    chans, first_steps,
    rate_ref, beam_ref, time_ref, mix_ref, turn_a_ref, turn_b_ref, before_ref, after_ref, shift_ref,
    out_ref, grid_ref, power_ref, scaled_ref,
):
    step = pl.program_id(0)
    samples = turn_a_ref.shape[1]
    low, comb = 2 * samples, grid_ref.shape[0]
    combs = beam_ref.shape[1]

    @pl.when(step == 0)
    def _():
        power_ref[...] = jnp.zeros_like(power_ref)

    @pl.when(step < first_steps)
    def _():
        for i in range(combs):
            beam = beam_ref[:, i].reshape(low, 2 * samples)
            wide = beam.astype(F32)
            power_ref[...] += jnp.sum((wide * wide).reshape(low // 8, 8, 2 * samples), 0)
            spectrum = jnp.dot(beam, time_ref[...], preferred_element_type=F32)
            comb_row = step * combs + i
            turned = cmul(
                (turn_a_ref[0], turn_a_ref[1]),
                (turn_b_ref[0, pl.ds(comb_row, 1), :], turn_b_ref[1, pl.ds(comb_row, 1), :]),
            )
            halves = []
            for h in range(2):
                piece = spectrum[h * samples : (h + 1) * samples]
                moved = cmul((piece[:, :samples], piece[:, samples:]), turned)
                halves.append(jnp.concatenate(moved, 1).astype(BF16))
            mixed = jnp.dot(
                mix_ref[i], jnp.concatenate(halves, 0), preferred_element_type=F32
            )
            grid_ref[comb_row, 0] = mixed[:low, :samples] - mixed[low:, samples:]
            grid_ref[comb_row, 1] = mixed[:low, samples:] + mixed[low:, :samples]

    @pl.when(step == first_steps)
    def _():
        mean_power = jnp.sum(power_ref[...]) / (samples * chans)
        factor = lax.rsqrt(jnp.full((1, samples), mean_power, F32) + EPSILON)
        for beta in range(2):
            for p in range(2):
                scaled_ref[beta, p] = after_ref[beta, p] * factor
        rate = 2 * rate_ref[0] + 1

        @pl.loop(0, low // 8)
        def _(tile):
            rows = pl.ds(pl.multiple_of(tile * 8, 8), 8)
            values = [(grid_ref[c, 0, rows, :], grid_ref[c, 1, rows, :]) for c in range(comb)]
            values = fft_list(values, 1)
            position = tile * 8 + lax.broadcasted_iota(jnp.int32, (8, samples), 0)
            wrapped = position < shift_ref[...]
            for m in range(comb):
                table = [
                    jnp.where(wrapped, before_ref[1, p, m : m + 1, :], before_ref[0, p, m : m + 1, :])
                    for p in range(2)
                ]
                values[m] = cmul(values[m], table)
            values = fft_list(values, -1)
            for k in range(comb):
                table = [
                    jnp.where(wrapped, scaled_ref[1, p, k : k + 1, :], scaled_ref[0, p, k : k + 1, :])
                    for p in range(2)
                ]
                real, imag = cmul(values[k], table)
                place = lax.rem(rate * k, comb)
                grid_ref[place, 0, rows, :] = real
                grid_ref[place, 1, rows, :] = imag

    @pl.when(step >= first_steps)
    def _():
        per = out_ref.shape[3] // low
        for i in range(per):
            high = (step - first_steps) * per + i
            both = jnp.concatenate([grid_ref[high, 0], grid_ref[high, 1]], 1).astype(BF16)
            result = lax.dot_general(
                time_ref[...], both, (((1,), (1,)), ((), ())), preferred_element_type=F32
            )
            out_ref[0, 0, :, i * low : (i + 1) * low] = result[:samples]
            out_ref[0, 1, :, i * low : (i + 1) * low] = result[samples:]


def dedisperse(beam, trial, samples, chans):
    low, comb = 2 * samples, chans // (2 * samples)
    tables = chirp_tables(2 * trial[0] + 1, samples, chans)
    time_mat, mix = transforms(samples, chans)
    devices, _, part_rows, width = beam.shape
    combs, first_steps, last_steps = 2, comb // 2, 4

    def early(i):
        return jnp.minimum(i, first_steps - 1)

    def whole(array):
        return pl.BlockSpec(array.shape, lambda i: (0,) * array.ndim)

    return pl.pallas_call(
        functools.partial(dedisperse_kernel, chans, first_steps),
        out_shape=jax.ShapeDtypeStruct((1, 2, samples, chans), F32),
        grid=(first_steps + last_steps,),
        in_specs=[
            pl.BlockSpec(memory_space=pltpu.SMEM),
            pl.BlockSpec((devices, combs, part_rows, width), lambda i: (0, early(i), 0, 0)),
            whole(time_mat),
            pl.BlockSpec((combs, 2 * low, low), lambda i: (early(i), 0, 0)),
        ]
        + [whole(table) for table in tables],
        out_specs=pl.BlockSpec(
            (1, 2, samples, chans // last_steps),
            lambda i: (0, 0, 0, jnp.maximum(i - first_steps, 0)),
        ),
        scratch_shapes=[
            pltpu.VMEM((comb, 2, low, samples), F32),
            pltpu.VMEM((8, 2 * samples), F32),
            pltpu.VMEM((2, 2, comb, samples), F32),
        ],
        compiler_params=pltpu.CompilerParams(vmem_limit_bytes=40 * 2**20),
        name="dedisperse",
    )(trial, beam, time_mat, mix, *tables)


def on_device(chan_devs, voltages, delays, pointing, dm_index, dish_mask):
    chan_dev, _, _, samples = voltages.shape
    chans = chan_dev * chan_devs
    comb = chans // (2 * samples)
    beam_dev = dm_index.shape[0]
    formed = form_beams(voltages, delays, pointing, dish_mask, chans, comb)
    formed = lax.all_to_all(formed, "chan", split_axis=0, concat_axis=0, tiled=True)
    part_rows = chan_dev // comb
    formed = formed.reshape(chan_devs, beam_dev, comb, part_rows, 2 * samples)
    if part_rows % 16:
        formed = jnp.transpose(formed, (1, 2, 0, 3, 4)).reshape(
            1, beam_dev, comb, chans // comb, 2 * samples
        )
    pieces = [
        dedisperse(formed[:, b], dm_index[b : b + 1], samples, chans) for b in range(beam_dev)
    ]
    return pieces[0] if beam_dev == 1 else jnp.concatenate(pieces, 0)


def solution(mesh):
    return jax.shard_map(
        functools.partial(on_device, mesh.shape["chan"]),
        mesh=mesh,
        in_specs=(
            P(("grp", "chan"), None, None, None),
            P(),
            P("grp"),
            P(("grp", "chan")),
            P("grp"),
        ),
        out_specs=P(("grp", "chan"), None, None, None),
        check_vma=False,
    )
```

profile of v0, /device:TPU:13, one launch (start us, length us, event | category | flops | bytes accessed | tf_op | source)
XLA Modules:
  0.0 79.5 jit_solution(14752197797913594721)
XLA Ops:
  0.0 0.0 copy-start.1
  0.0 3.4 %copy-done.1 = bf16[256,2,64,128]{3,2,1,0:T(8,128)(2,1)S(1)} copy-done((bf16[256,2,64,128]{3,2,1,0:T(8,128)(2,1)S(1)}, bf16[256,2,64,128]{3,2,1,0:T(8,128)(2,1)}, u32[]{:S(2)}) %copy-start.1) | copy-done | bytes 8388632
  3.4 0.0 copy-start.3
  3.4 0.9 %copy-done.3 = f32[512,64]{0,1:T(8,128)S(1)} copy-done((f32[512,64]{0,1:T(8,128)S(1)}, f32[512,64]{0,1:T(8,128)}, u32[]{:S(2)}) %copy-start.3) | copy-done | bytes 131096
  4.3 0.0 copy-start.4
  4.3 0.7 copy-done.4
  4.9 0.0 copy-start.5
  4.9 0.7 copy-done.5
  5.6 5.3 %form_beams.1 = bf16[16,256,256]{2,1,0:T(8,128)(2,1)S(1)} custom-call(s32[16]{0:T(128)S(1)} %copy-done.4, f32[64,512]{1,0:T(8,128)S(1)} %bitcast.17, s32[1,64]{1,0:T(1,128)S(1)} %bitcast.18, bf16[16,16,128,128]{3,2,1,0:T(8,128)(2,1)S(1)} %bitcast.15), custom_call_target="tpu_custom_call" | custom-call | tf_op jit(solution)/shard_map/form_beams/pallas_call | solution.py:144
  10.9 0.0 copy-start.2
  10.9 1.3 %copy-done.2 = bf16[16,256,256]{2,1,0:T(8,128)(2,1)} copy-done((bf16[16,256,256]{2,1,0:T(8,128)(2,1)}, bf16[16,256,256]{2,1,0:T(8,128)(2,1)S(1)}, u32[]{:S(2)}) %copy-start.2) | copy-done | bytes 2097176
  12.2 6.6 %all-to-all-start = ((bf16[16,256,256]{2,1,0:T(8,128)(2,1)}), bf16[16,256,256]{2,1,0:T(8,128)(2,1)S(1)}, u32[]{:S(2)}, u32[]{:S(2)}) async-start(bf16[16,256,256]{2,1,0:T(8,128)(2,1)} %copy-done.2), calls=%async_computation | async-start | bytes 4194304 | tf_op jit(solution)/shard_map/all_to_all | solution.py:342
  19.5 0.1 fusion.96
  19.6 0.1 maximum_reduce_fusion
  19.7 0.6 fusion.98
  21.6 0.1 fusion.78
  21.7 0.2 multiply_subtract_fusion.1
  21.9 0.2 fusion.72
  22.1 0.3 fusion.31
  22.4 0.3 negate_convert_fusion
  22.7 0.4 fusion.29
  23.2 19.4 %cosine_convert_fusion = (bf16[16,256,256]{2,1,0:T(8,128)(2,1)S(1)}, bf16[16,256,256]{2,1,0:T(8,128)(2,1)S(1)}) fusion(s32[16,256]{1,0:T(8,128)S(1)} %iota_add_fusion), kind=kLoop, calls=%fused_computation.14 | loop fusion | flops 30408704 | bytes 4210688 | tf_op jit(solution)/shard_map/convert
  42.6 2.4 %pad_maximum_fusion.mix_ref = bf16[16,512,256]{2,1,0:T(8,128)(2,1)} fusion(bf16[16,256,256]{2,1,0:T(8,128)(2,1)S(1)} %get-tuple-element.6, bf16[16,256,256]{2,1,0:T(8,128)(2,1)S(1)} %get-tuple-element.5), kind=kLoop, calls=%fused_computation.12 | loop fusion | flops 8388608 | bytes 8388608 | tf_op jit(solution)/shard_map/concatenate | solution.py:212
  45.0 21.2 %all-to-all-done = bf16[16,256,256]{2,1,0:T(8,128)(2,1)S(1)} async-done(((bf16[16,256,256]{2,1,0:T(8,128)(2,1)}), bf16[16,256,256]{2,1,0:T(8,128)(2,1)S(1)}, u32[]{:S(2)}, u32[]{:S(2)}) %all-to-all-start) | async-done | bytes 2097184 | tf_op jit(solution)/shard_map/all_to_all | solution.py:342
  66.2 0.0 copy-start
  66.2 2.2 %copy-done = bf16[16,512,256]{2,1,0:T(8,128)(2,1)S(1)} copy-done((bf16[16,512,256]{2,1,0:T(8,128)(2,1)S(1)}, bf16[16,512,256]{2,1,0:T(8,128)(2,1)}, u32[]{:S(2)}) %copy-start) | copy-done | bytes 4194328
  68.4 11.1 %dedisperse.1 = f32[1,2,128,4096]{3,2,1,0:T(8,128)} custom-call(s32[1]{0:T(128)S(6)} %copy.6.rate_ref, bf16[16,16,16,256]{3,2,1,0:T(8,128)(2,1)S(1)} %bitcast.16, bf16[256,256]{1,0:T(8,128)(2,1)S(1)} %maximum_maximum_fusion.time_ref, bf16[16,512,256]{2,1,0:T(8,128)(2,1)S(1)} %copy-done, f32[2,128,128]{2,1,0:T(8,128)S(1)} %pad_maximum_fusion.1.turn_a_ref, ...), custom_call_target="tpu_custom_call" | custom-call | tf_op jit(solution)/shard_map/dedisperse/pallas_call | solution.py:311
  (19 shorter events, 0.2 us)
Async XLA Ops:
  0.0 3.4 %copy-start.1 = (bf16[256,2,64,128]{3,2,1,0:T(8,128)(2,1)S(1)}, bf16[256,2,64,128]{3,2,1,0:T(8,128)(2,1)}, u32[]{:S(2)}) copy-start(bf16[256,2,64,128]{3,2,1,0:T(8,128)(2,1)} %param.5) | copy-start | bytes 25165828
  3.4 0.9 %copy-start.3 = (f32[512,64]{0,1:T(8,128)S(1)}, f32[512,64]{0,1:T(8,128)}, u32[]{:S(2)}) copy-start(f32[512,64]{0,1:T(8,128)} %param.6) | copy-start | bytes 393220
  4.3 0.7 copy-start.4
  4.9 0.7 copy-start.5
  10.9 1.3 %copy-start.2 = (bf16[16,256,256]{2,1,0:T(8,128)(2,1)}, bf16[16,256,256]{2,1,0:T(8,128)(2,1)S(1)}, u32[]{:S(2)}) copy-start(bf16[16,256,256]{2,1,0:T(8,128)(2,1)S(1)} %form_beams.1) | copy-start | bytes 6291460
  12.2 54.0 %all-to-all-start = ((bf16[16,256,256]{2,1,0:T(8,128)(2,1)}), bf16[16,256,256]{2,1,0:T(8,128)(2,1)S(1)}, u32[]{:S(2)}, u32[]{:S(2)}) async-start(bf16[16,256,256]{2,1,0:T(8,128)(2,1)} %copy-done.2), calls=%async_computation | async-start | bytes 4194304 | tf_op jit(solution)/shard_map/all_to_all | solution.py:342
  66.2 2.2 %copy-start = (bf16[16,512,256]{2,1,0:T(8,128)(2,1)S(1)}, bf16[16,512,256]{2,1,0:T(8,128)(2,1)}, u32[]{:S(2)}) copy-start(bf16[16,512,256]{2,1,0:T(8,128)(2,1)} %pad_maximum_fusion.mix_ref) | copy-start | bytes 12582916
where the time goes:
time: 79.8 us; the launch traced here: 79.5 us
  other arithmetic  23.6 us (30%)
  waiting for transfers between devices  21.2 us (27%)
  Pallas kernels  16.4 us (21%)
  local copies, waits for them, and re-layouts  9.69 us (12%)
  starting transfers between devices  6.55 us (8%)
  between operations  2.02 us (3%)
    all_to_all x1, waiting for transfers between devices, on_device(): lax.all_to_all(formed, 'chan', split_axis=0, concat_axis=0, tiled=True)  21.2 us
    another operation x3, other arithmetic  20 us
    pallas_call x1, Pallas kernels, dedisperse(): pl.pallas_call(functools.partial(dedisperse_kernel, chans, first_steps),...  11.1 us
    unnamed x12, local copies, waits for them, and re-layouts  9.1 us
    all_to_all x1, starting transfers between devices, on_device(): lax.all_to_all(formed, 'chan', split_axis=0, concat_axis=0, tiled=True)  6.55 us
    pallas_call x1, Pallas kernels, form_beams(): pl.pallas_call(functools.partial(beam_kernel, chans, comb), out_shape=jax...  5.29 us
    concatenate x1, other arithmetic, transforms(): jnp.concatenate([cosine, sine], 1).astype(BF16)  2.4 us
  transfers between devices with their start and end apart: 1, of which 1 were waited for; matrix products, arithmetic and copies ran while one was open for 30% of the time, Pallas kernels for 0%

commit v1 on v0

--- a/solution.py
+++ b/solution.py
@@ -69,96 +69,120 @@
 
 
 def beam_kernel(
-    chans, comb, point_ref, delay_ref, mask_ref, volt_ref, out_ref, zero_ref, fine_ref, coarse_ref, rows_ref
+    chans, comb, point_ref, delay_hbm, mask_hbm, volt_hbm, out_hbm,
+    delay_ref, mask_ref, volt_ref, out_ref, zero_ref, fine_ref, coarse_ref, rows_ref,
+    small_sem, volt_sem, out_sem,
 ):
-    step = pl.program_id(0)
-    part_rows, combs = volt_ref.shape[0], volt_ref.shape[1]
+    part_rows = volt_ref.shape[0]
     beams = out_ref.shape[0]
     dishes = delay_ref.shape[0]
+    samples = rows_ref.shape[3]
     chan_dev = part_rows * comb
-
-    @pl.when(step == 0)
-    def _():
-        table_rows = delay_ref.shape[1]
-        place = lax.broadcasted_iota(jnp.int32, (beams, table_rows), 1)
-        which = lax.broadcasted_iota(jnp.int32, (beams, table_rows), 0)
-        wanted = jnp.zeros((beams, table_rows), jnp.int32)
-        for b in range(beams):
-            wanted = jnp.where(which == b, point_ref[b], wanted)
-        select = (wanted == place).astype(F32)
-        doubled = jnp.concatenate([delay_ref[...], delay_ref[...]], 0)
-        tau = lax.dot_general(
-            select,
-            doubled,
-            (((1,), (1,)), ((), ())),
-            precision=lax.Precision.HIGHEST,
-            preferred_element_type=F32,
-        )
-        first = lax.axis_index("chan") * chan_dev
-        frequency = BAND_LOW + BAND_WIDTH * (first.astype(F32) + 0.5) / chans
-        angle = (TWO_PI * frequency) * tau
-        gain_half = mask_ref[...].astype(F32) / math.sqrt(dishes)
-        gain = jnp.concatenate([gain_half, gain_half], 1)
-        cosine, sine = jnp.cos(angle) * gain, jnp.sin(angle) * gain
-        left = lax.broadcasted_iota(jnp.int32, (beams, 2 * dishes), 1) < dishes
-        zero_ref[0] = jnp.where(left, cosine, sine)
-        zero_ref[1] = jnp.where(left, -sine, cosine)
-        for table_ref, stride in ((fine_ref, 1), (coarse_ref, comb)):
-            shift = (TWO_PI * BAND_WIDTH / chans * stride) * tau
-            count = table_ref.shape[0]
-            powers = [(jnp.ones_like(tau), jnp.zeros_like(tau)), (jnp.cos(shift), -jnp.sin(shift))]
-            for k in range(2, count):
-                powers.append(cmul(powers[k // 2], powers[k - k // 2]))
-            for k in range(count):
-                table_ref[k, 0] = powers[k][0]
-                table_ref[k, 1] = powers[k][1]
-
-    group = rows_ref.shape[1] // beams
-    for g in range(part_rows * combs // group):
+    group = rows_ref.shape[2] // beams
+    group_combs = group // part_rows
+    groups = chan_dev // group
+
+    def volt_copy(g):
+        combs = pl.ds(g * group_combs, group_combs)
+        return pltpu.make_async_copy(volt_hbm.at[:, combs], volt_ref.at[:, combs], volt_sem.at[g])
+
+    def out_copy(g):
+        rows = pl.ds(pl.multiple_of(g * group, group), group)
+        return pltpu.make_async_copy(out_ref.at[:, rows], out_hbm.at[:, rows], out_sem.at[g])
+
+    delay_copy = pltpu.make_async_copy(delay_hbm, delay_ref, small_sem.at[0])
+    mask_copy = pltpu.make_async_copy(mask_hbm, mask_ref, small_sem.at[1])
+    delay_copy.start()
+    mask_copy.start()
+    for g in range(groups):
+        volt_copy(g).start()
+    delay_copy.wait()
+    mask_copy.wait()
+
+    table_rows = delay_ref.shape[1]
+    place = lax.broadcasted_iota(jnp.int32, (beams, table_rows), 1)
+    which = lax.broadcasted_iota(jnp.int32, (beams, table_rows), 0)
+    wanted = jnp.zeros((beams, table_rows), jnp.int32)
+    for b in range(beams):
+        wanted = jnp.where(which == b, point_ref[b], wanted)
+    select = (wanted == place).astype(F32)
+    doubled = jnp.concatenate([delay_ref[...], delay_ref[...]], 0)
+    tau = lax.dot_general(
+        select,
+        doubled,
+        (((1,), (1,)), ((), ())),
+        precision=lax.Precision.HIGHEST,
+        preferred_element_type=F32,
+    )
+    first = lax.axis_index("chan") * chan_dev
+    frequency = BAND_LOW + BAND_WIDTH * (first.astype(F32) + 0.5) / chans
+    angle = (TWO_PI * frequency) * tau
+    gain_half = mask_ref[...].astype(F32) / math.sqrt(dishes)
+    gain = jnp.concatenate([gain_half, gain_half], 1)
+    cosine, sine = jnp.cos(angle) * gain, jnp.sin(angle) * gain
+    left = lax.broadcasted_iota(jnp.int32, (beams, 2 * dishes), 1) < dishes
+    zero_ref[0] = jnp.where(left, cosine, sine)
+    zero_ref[1] = jnp.where(left, -sine, cosine)
+    for table_ref, stride in ((fine_ref, 1), (coarse_ref, comb)):
+        shift = (TWO_PI * BAND_WIDTH / chans * stride) * tau
+        count = table_ref.shape[0]
+        powers = [(jnp.ones_like(tau), jnp.zeros_like(tau)), (jnp.cos(shift), -jnp.sin(shift))]
+        for k in range(2, count):
+            powers.append(cmul(powers[k // 2], powers[k - k // 2]))
+        for k in range(count):
+            table_ref[k, 0] = powers[k][0]
+            table_ref[k, 1] = powers[k][1]
+
+    @pl.loop(0, groups)
+    def _(g):
+        volt_copy(g).wait()
+        slot = g % 2
         for i in range(group):
-            row = g * group + i
-            ja, cb = row % part_rows, row // part_rows
-            base = cmul(
-                (zero_ref[0], zero_ref[1]),
-                (fine_ref[step * combs + cb, 0], fine_ref[step * combs + cb, 1]),
-            )
+            ja, cb = i % part_rows, g * group_combs + i // part_rows
+            if ja == 0:
+                base = cmul((zero_ref[0], zero_ref[1]), (fine_ref[cb, 0], fine_ref[cb, 1]))
             weight = cmul(base, (coarse_ref[ja, 0], coarse_ref[ja, 1]))
             stacked = jnp.concatenate(weight, 0).astype(BF16)
             formed = jnp.dot(stacked, volt_ref[ja, cb], preferred_element_type=F32)
-            rows_ref[0, pl.ds(i, beams, stride=group), :] = formed[:beams]
-            rows_ref[1, pl.ds(i, beams, stride=group), :] = formed[beams:]
-        samples = rows_ref.shape[2]
+            rows_ref[slot, 0, pl.ds(i, beams, stride=group), :] = formed[:beams]
+            rows_ref[slot, 1, pl.ds(i, beams, stride=group), :] = formed[beams:]
+        rows = pl.ds(pl.multiple_of(g * group, group), group)
         for p in range(2):
-            out_ref[:, g * group : (g + 1) * group, p * samples : (p + 1) * samples] = (
-                rows_ref[p].reshape(beams, group, samples).astype(BF16)
+            out_ref[:, rows, p * samples : (p + 1) * samples] = (
+                rows_ref[slot, p].reshape(beams, group, samples).astype(BF16)
             )
+        out_copy(g).start()
+
+    for g in range(groups):
+        out_copy(g).wait()
 
 
 def form_beams(voltages, delays, pointing, dish_mask, chans, comb):
     chan_dev, _, dishes, samples = voltages.shape
     beams = pointing.shape[0]
     part_rows = chan_dev // comb
-    combs = max(2, 16 // part_rows)
-    group = 16
+    group = part_rows * max(1, 16 // part_rows)
+    hbm = pl.BlockSpec(memory_space=pltpu.HBM)
     volt = voltages.reshape(part_rows, comb, 2 * dishes, samples)
     return pl.pallas_call(
         functools.partial(beam_kernel, chans, comb),
         out_shape=jax.ShapeDtypeStruct((beams, chan_dev, 2 * samples), BF16),
-        grid=(comb // combs,),
-        in_specs=[
-            pl.BlockSpec(memory_space=pltpu.SMEM),
-            pl.BlockSpec((dishes, delays.shape[0]), lambda i: (0, 0)),
-            pl.BlockSpec((1, dishes), lambda i: (0, 0)),
-            pl.BlockSpec((part_rows, combs, 2 * dishes, samples), lambda i: (0, i, 0, 0)),
-        ],
-        out_specs=pl.BlockSpec((beams, part_rows * combs, 2 * samples), lambda i: (0, i, 0)),
+        in_specs=[pl.BlockSpec(memory_space=pltpu.SMEM), hbm, hbm, hbm],
+        out_specs=hbm,
         scratch_shapes=[
+            pltpu.VMEM((dishes, delays.shape[0]), F32),
+            pltpu.VMEM((1, dishes), jnp.int32),
+            pltpu.VMEM(volt.shape, BF16),
+            pltpu.VMEM((beams, chan_dev, 2 * samples), BF16),
             pltpu.VMEM((2, beams, 2 * dishes), F32),
             pltpu.VMEM((comb, 2, beams, 2 * dishes), F32),
             pltpu.VMEM((part_rows, 2, beams, 2 * dishes), F32),
-            pltpu.VMEM((2, beams * group, samples), F32),
+            pltpu.VMEM((2, 2, beams * group, samples), F32),
+            pltpu.SemaphoreType.DMA((2,)),
+            pltpu.SemaphoreType.DMA((chan_dev // group,)),
+            pltpu.SemaphoreType.DMA((chan_dev // group,)),
         ],
-        compiler_params=pltpu.CompilerParams(vmem_limit_bytes=40 * 2**20),
+        compiler_params=pltpu.CompilerParams(vmem_limit_bytes=60 * 2**20),
         name="form_beams",
     )(pointing, delays.T, dish_mask.reshape(1, dishes), volt)
 
@@ -198,42 +222,50 @@
     return turn_a, turn_b, jnp.stack(before), jnp.stack(after), shift_low
 
 
-def transforms(samples, chans):
-    low, comb = 2 * samples, chans // (2 * samples)
+def time_matrix(samples):
     t = jnp.arange(samples, dtype=jnp.int32)
     cosine, sine = phasor(t[:, None] * t[None, :] % samples, samples)
-    time_mat = jnp.concatenate(
+    return jnp.concatenate(
         [jnp.concatenate([cosine, -sine], 1), jnp.concatenate([sine, cosine], 1)], 0
-    )
+    ).astype(BF16)
+
+
+def mix_matrices(samples, chans):
+    low, comb = 2 * samples, chans // (2 * samples)
     n = jnp.arange(low, dtype=jnp.int32)
     c_b = jnp.arange(comb, dtype=jnp.int32)
     product = (comb * n[None, None, :] + c_b[:, None, None]) * n[None, :, None] % chans
     cosine, sine = phasor(product, chans)
-    return time_mat.astype(BF16), jnp.concatenate([cosine, sine], 1).astype(BF16)
+    return jnp.concatenate([cosine, sine], 1).astype(BF16)
 
 
 def dedisperse_kernel(
     chans, first_steps,
-    rate_ref, beam_ref, time_ref, mix_ref, turn_a_ref, turn_b_ref, before_ref, after_ref, shift_ref,
-    out_ref, grid_ref, power_ref, scaled_ref,
+    rate_ref, beam_ref, time_ref, mix_hbm, turn_a_ref, turn_b_ref, before_ref, after_ref, shift_ref,
+    out_ref, grid_ref, power_ref, scaled_ref, mix_ref, mix_sem,
 ):
     step = pl.program_id(0)
     samples = turn_a_ref.shape[1]
     low, comb = 2 * samples, grid_ref.shape[0]
-    combs = beam_ref.shape[1]
+    combs = comb // first_steps
+
+    def mix_copy(c):
+        return pltpu.make_async_copy(mix_hbm.at[c], mix_ref.at[c], mix_sem.at[c])
 
     @pl.when(step == 0)
     def _():
+        for c in range(comb):
+            mix_copy(c).start()
         power_ref[...] = jnp.zeros_like(power_ref)
 
     @pl.when(step < first_steps)
     def _():
         for i in range(combs):
-            beam = beam_ref[:, i].reshape(low, 2 * samples)
+            comb_row = step * combs + i
+            beam = beam_ref[:, comb_row].reshape(low, 2 * samples)
             wide = beam.astype(F32)
             power_ref[...] += jnp.sum((wide * wide).reshape(low // 8, 8, 2 * samples), 0)
             spectrum = jnp.dot(beam, time_ref[...], preferred_element_type=F32)
-            comb_row = step * combs + i
             turned = cmul(
                 (turn_a_ref[0], turn_a_ref[1]),
                 (turn_b_ref[0, pl.ds(comb_row, 1), :], turn_b_ref[1, pl.ds(comb_row, 1), :]),
@@ -243,9 +275,9 @@
                 piece = spectrum[h * samples : (h + 1) * samples]
                 moved = cmul((piece[:, :samples], piece[:, samples:]), turned)
                 halves.append(jnp.concatenate(moved, 1).astype(BF16))
-            mixed = jnp.dot(
-                mix_ref[i], jnp.concatenate(halves, 0), preferred_element_type=F32
-            )
+            moved = jnp.concatenate(halves, 0)
+            mix_copy(comb_row).wait()
+            mixed = jnp.dot(mix_ref[comb_row], moved, preferred_element_type=F32)
             grid_ref[comb_row, 0] = mixed[:low, :samples] - mixed[low:, samples:]
             grid_ref[comb_row, 1] = mixed[:low, samples:] + mixed[low:, :samples]
 
@@ -298,27 +330,16 @@
 def dedisperse(beam, trial, samples, chans):
     low, comb = 2 * samples, chans // (2 * samples)
     tables = chirp_tables(2 * trial[0] + 1, samples, chans)
-    time_mat, mix = transforms(samples, chans)
-    devices, _, part_rows, width = beam.shape
-    combs, first_steps, last_steps = 2, comb // 2, 4
-
-    def early(i):
-        return jnp.minimum(i, first_steps - 1)
-
-    def whole(array):
-        return pl.BlockSpec(array.shape, lambda i: (0,) * array.ndim)
-
+    time_mat = time_matrix(samples)
+    mix = mix_matrices(samples, chans)
+    first_steps, last_steps = comb // 2, 4
+    vmem = pl.BlockSpec(memory_space=pltpu.VMEM)
     return pl.pallas_call(
         functools.partial(dedisperse_kernel, chans, first_steps),
         out_shape=jax.ShapeDtypeStruct((1, 2, samples, chans), F32),
         grid=(first_steps + last_steps,),
-        in_specs=[
-            pl.BlockSpec(memory_space=pltpu.SMEM),
-            pl.BlockSpec((devices, combs, part_rows, width), lambda i: (0, early(i), 0, 0)),
-            whole(time_mat),
-            pl.BlockSpec((combs, 2 * low, low), lambda i: (early(i), 0, 0)),
-        ]
-        + [whole(table) for table in tables],
+        in_specs=[pl.BlockSpec(memory_space=pltpu.SMEM), vmem, vmem, pl.BlockSpec(memory_space=pl.ANY)]
+        + [vmem] * len(tables),
         out_specs=pl.BlockSpec(
             (1, 2, samples, chans // last_steps),
             lambda i: (0, 0, 0, jnp.maximum(i - first_steps, 0)),
@@ -327,8 +348,10 @@
             pltpu.VMEM((comb, 2, low, samples), F32),
             pltpu.VMEM((8, 2 * samples), F32),
             pltpu.VMEM((2, 2, comb, samples), F32),
+            pltpu.VMEM(mix.shape, BF16),
+            pltpu.SemaphoreType.DMA((comb,)),
         ],
-        compiler_params=pltpu.CompilerParams(vmem_limit_bytes=40 * 2**20),
+        compiler_params=pltpu.CompilerParams(vmem_limit_bytes=50 * 2**20),
         name="dedisperse",
     )(trial, beam, time_mat, mix, *tables)
 

time: 79.8 us -> 77.9 us (0.976)
  local copies, waits for them, and re-layouts: 9.69 us -> 0.59 us
  Pallas kernels: 16.4 us -> 23.7 us
    unnamed x12 -> x0, local copies, waits for them, and re-layouts: 9.1 us -> none
    pallas_call x1, Pallas kernels: 5.29 us -> 9.67 us  [form_beams(): pl.pallas_call(functools.partial(beam_kernel, chans, comb), out_shape=jax...]
    pallas_call x1, Pallas kernels: 11.1 us -> 14 us  [dedisperse(): pl.pallas_call(functools.partial(dedisperse_kernel, chans, first_steps),...]
  transfers between devices with their start and end apart: 1 -> 1, of which waited for: 1 -> 1; matrix products, arithmetic and copies ran while one was open for 30% -> 31% of each run, Pallas kernels for 0% -> 0%
where the time goes in v1:
time: 77.9 us; the launch traced here: 77.7 us
  Pallas kernels  23.7 us (30%)
  other arithmetic  23.6 us (30%)
  waiting for transfers between devices  21.3 us (27%)
  starting transfers between devices  6.57 us (8%)
  between operations  2.02 us (3%)
    all_to_all x1, waiting for transfers between devices, on_device(): lax.all_to_all(formed, 'chan', split_axis=0, concat_axis=0, tiled=True)  21.3 us
    another operation x3, other arithmetic  20 us
    pallas_call x1, Pallas kernels, dedisperse(): pl.pallas_call(functools.partial(dedisperse_kernel, chans, first_steps),...  14 us
    pallas_call x1, Pallas kernels, form_beams(): pl.pallas_call(functools.partial(beam_kernel, chans, comb), out_shape=jax...  9.67 us
    all_to_all x1, starting transfers between devices, on_device(): lax.all_to_all(formed, 'chan', split_axis=0, concat_axis=0, tiled=True)  6.57 us
    concatenate x1, other arithmetic, mix_matrices(): return jnp.concatenate([cosine, sine], 1).astype(BF16)  2.34 us
  transfers between devices with their start and end apart: 1, of which 1 were waited for; matrix products, arithmetic and copies ran while one was open for 31% of the time, Pallas kernels for 0%

profile of v1, /device:TPU:13, one launch (start us, length us, event | category | flops | bytes accessed | tf_op | source)
XLA Modules:
  0.0 77.7 jit_solution(8323852357374311003)
XLA Ops:
  0.0 9.7 %form_beams.1 = bf16[16,256,256]{2,1,0:T(8,128)(2,1)} custom-call(s32[16]{0:T(128)} %point_ref.1, f32[64,512]{1,0:T(8,128)} %bitcast.17, s32[1,64]{1,0:T(1,128)} %bitcast.18, bf16[16,16,128,128]{3,2,1,0:T(8,128)(2,1)} %bitcast.16), custom_call_target="tpu_custom_call" | custom-call | tf_op jit(solution)/shard_map/form_beams/pallas_call | solution.py:167
  9.7 6.6 %all-to-all-start = ((bf16[16,256,256]{2,1,0:T(8,128)(2,1)}), bf16[16,256,256]{2,1,0:T(8,128)(2,1)S(1)}, u32[]{:S(2)}, u32[]{:S(2)}) async-start(bf16[16,256,256]{2,1,0:T(8,128)(2,1)} %form_beams.1), calls=%async_computation | async-start | bytes 4194304 | tf_op jit(solution)/shard_map/all_to_all | solution.py:365
  17.0 0.1 fusion.96
  17.1 0.1 maximum_reduce_fusion
  17.2 0.6 fusion.98
  19.1 0.1 fusion.78
  19.2 0.2 multiply_subtract_fusion.1
  19.4 0.2 fusion.72
  19.6 0.3 fusion.31
  19.9 0.3 negate_convert_fusion
  20.2 0.4 fusion.29
  20.6 19.4 %cosine_convert_fusion = (bf16[16,256,256]{2,1,0:T(8,128)(2,1)S(1)}, bf16[16,256,256]{2,1,0:T(8,128)(2,1)S(1)}) fusion(s32[16,256]{1,0:T(8,128)S(1)} %iota_add_fusion), kind=kLoop, calls=%fused_computation.14 | loop fusion | flops 30408704 | bytes 4210688 | tf_op jit(solution)/shard_map/convert
  40.1 2.3 %pad_maximum_fusion.mix_hbm = bf16[16,512,256]{2,1,0:T(8,128)(2,1)} fusion(bf16[16,256,256]{2,1,0:T(8,128)(2,1)S(1)} %get-tuple-element.6, bf16[16,256,256]{2,1,0:T(8,128)(2,1)S(1)} %get-tuple-element.5), kind=kLoop, calls=%fused_computation.12 | loop fusion | flops 8388608 | bytes 8388608 | tf_op jit(solution)/shard_map/concatenate | solution.py:239
  42.4 21.3 %all-to-all-done = bf16[16,256,256]{2,1,0:T(8,128)(2,1)S(1)} async-done(((bf16[16,256,256]{2,1,0:T(8,128)(2,1)}), bf16[16,256,256]{2,1,0:T(8,128)(2,1)S(1)}, u32[]{:S(2)}, u32[]{:S(2)}) %all-to-all-start) | async-done | bytes 2097184 | tf_op jit(solution)/shard_map/all_to_all | solution.py:365
  63.7 14.0 %dedisperse.1 = f32[1,2,128,4096]{3,2,1,0:T(8,128)} custom-call(s32[1]{0:T(128)S(6)} %copy.6.rate_ref, bf16[16,16,16,256]{3,2,1,0:T(8,128)(2,1)S(1)} %bitcast.15, bf16[256,256]{1,0:T(8,128)(2,1)S(1)} %maximum_maximum_fusion.time_ref, bf16[16,512,256]{2,1,0:T(8,128)(2,1)} %pad_maximum_fusion.mix_hbm, f32[2,128,128]{2,1,0:T(8,128)S(1)} %pad_maximum_fusion.1.turn_a_ref, ...), custom_call_target="tpu_custom_call" | custom-call | tf_op jit(solution)/shard_map/dedisperse/pallas_call | solution.py:337
  (19 shorter events, 0.2 us)
Async XLA Ops:
  9.7 54.0 %all-to-all-start = ((bf16[16,256,256]{2,1,0:T(8,128)(2,1)}), bf16[16,256,256]{2,1,0:T(8,128)(2,1)S(1)}, u32[]{:S(2)}, u32[]{:S(2)}) async-start(bf16[16,256,256]{2,1,0:T(8,128)(2,1)} %form_beams.1), calls=%async_computation | async-start | bytes 4194304 | tf_op jit(solution)/shard_map/all_to_all | solution.py:365

commit v2 on v1

v2 whole, which is shorter than its diff:
```python
import functools
import math

import jax
import jax.numpy as jnp
from jax import lax
from jax.experimental import pallas as pl
from jax.experimental.pallas import tpu as pltpu
from jax.sharding import PartitionSpec as P

TWO_PI = 2.0 * math.pi
BAND_LOW = 0.856
BAND_WIDTH = 0.856
EPSILON = 1e-06
F32 = jnp.float32
BF16 = jnp.bfloat16


def cmul(a, b):
    return (a[0] * b[0] - a[1] * b[1], a[0] * b[1] + a[1] * b[0])


def cadd(a, b):
    return (a[0] + b[0], a[1] + b[1])


def csub(a, b):
    return (a[0] - b[0], a[1] - b[1])


def turn(a, num, den):
    num = num % den
    if num == 0:
        return a
    if 2 * num == den:
        return (-a[0], -a[1])
    if 4 * num == den:
        return (-a[1], a[0])
    if 4 * num == 3 * den:
        return (a[1], -a[0])
    if 8 * num % den == 0:
        root = math.sqrt(0.5)
        plus, minus = (a[0] + a[1]) * root, (a[0] - a[1]) * root
        return {1: (minus, plus), 3: (-plus, minus), 5: (-minus, -plus), 7: (plus, -minus)}[
            8 * num // den
        ]
    cosine, sine = math.cos(TWO_PI * num / den), math.sin(TWO_PI * num / den)
    return (a[0] * cosine - a[1] * sine, a[0] * sine + a[1] * cosine)


def fft_list(values, sign):
    points = len(values)
    if points == 1:
        return values
    if points == 2:
        return [cadd(values[0], values[1]), csub(values[0], values[1])]
    quarter = points // 4
    parts = [fft_list(values[i::4], sign) for i in range(4)]
    out = [None] * points
    for k in range(quarter):
        a, b, c, d = [turn(parts[i][k], sign * i * k, points) for i in range(4)]
        s0, s1 = cadd(a, c), csub(a, c)
        s2, s3 = cadd(b, d), turn(csub(b, d), sign, 4)
        out[k] = cadd(s0, s2)
        out[k + quarter] = cadd(s1, s3)
        out[k + 2 * quarter] = csub(s0, s2)
        out[k + 3 * quarter] = csub(s1, s3)
    return out


def small_phasor(x):
    y = x * x
    cosine = 1.0 - y * (1 / 2 - y * (1 / 24 - y * (1 / 720)))
    return cosine, x * (1.0 - y * (1 / 6 - y * (1 / 120 - y * (1 / 5040))))


def wide_phasor(x):
    quarter = jnp.floor(x * (2.0 / math.pi) + 0.5)
    rest = x - quarter * 1.5703125
    rest = rest - quarter * 4.837512969970703125e-4
    rest = rest - quarter * 7.54978995489188e-8
    y = rest * rest
    cosine = 1.0 - y * (0.5 - y * (1 / 24 - y * (1 / 720 - y * (1 / 40320))))
    sine = rest * (1.0 - y * (1 / 6 - y * (1 / 120 - y * (1 / 5040 - y * (1 / 362880)))))
    turns = quarter.astype(jnp.int32)
    swap = (turns & 1) == 1
    even, odd = jnp.where(swap, sine, cosine), jnp.where(swap, cosine, sine)
    return (
        jnp.where(((turns + 1) & 2) == 2, -even, even),
        jnp.where((turns & 2) == 2, -odd, odd),
    )


def beam_kernel(
    chans, comb, point_ref, delay_hbm, mask_hbm, volt_hbm, out_hbm,
    delay_ref, mask_ref, volt_ref, out_ref, zero_ref, fine_ref, coarse_ref, rows_ref,
    small_sem, volt_sem, out_sem,
):
    part_rows = volt_ref.shape[0]
    beams = out_ref.shape[0]
    dishes = delay_ref.shape[0]
    samples = rows_ref.shape[3]
    chan_dev = part_rows * comb
    group = rows_ref.shape[2] // beams
    group_combs = group // part_rows
    groups = chan_dev // group
    chunks = volt_sem.shape[0]
    per = groups // chunks

    def volt_copy(g):
        combs = pl.ds(g * per * group_combs, per * group_combs)
        return pltpu.make_async_copy(volt_hbm.at[:, combs], volt_ref.at[:, combs], volt_sem.at[g])

    def out_copy(g):
        rows = pl.ds(g * per * group, per * group)
        return pltpu.make_async_copy(out_ref.at[:, rows], out_hbm.at[:, rows], out_sem.at[g])

    delay_copy = pltpu.make_async_copy(delay_hbm, delay_ref, small_sem.at[0])
    mask_copy = pltpu.make_async_copy(mask_hbm, mask_ref, small_sem.at[1])
    delay_copy.start()
    mask_copy.start()
    for g in range(chunks):
        volt_copy(g).start()
    delay_copy.wait()
    mask_copy.wait()

    table_rows = delay_ref.shape[1]
    place = lax.broadcasted_iota(jnp.int32, (beams, table_rows), 1)
    which = lax.broadcasted_iota(jnp.int32, (beams, table_rows), 0)
    wanted = jnp.zeros((beams, table_rows), jnp.int32)
    for b in range(beams):
        wanted = jnp.where(which == b, point_ref[b], wanted)
    select = (wanted == place).astype(F32).astype(BF16)
    rest, pieces = delay_ref[...], []
    for _ in range(3):
        piece = rest.astype(BF16)
        rest = rest - piece.astype(F32)
        pieces += [piece, piece]
    found = lax.dot_general(
        select,
        jnp.concatenate(pieces, 0),
        (((1,), (1,)), ((), ())),
        preferred_element_type=F32,
    )
    width = 2 * dishes
    tau = (found[:, 2 * width :] + found[:, width : 2 * width]) + found[:, :width]
    first = lax.axis_index("chan") * chan_dev
    frequency = BAND_LOW + BAND_WIDTH * (first.astype(F32) + 0.5) / chans
    angle = (TWO_PI * frequency) * tau
    gain_half = mask_ref[...].astype(F32) / math.sqrt(dishes)
    gain = jnp.concatenate([gain_half, gain_half], 1)
    cosine, sine = wide_phasor(angle)
    cosine, sine = cosine * gain, sine * gain
    left = lax.broadcasted_iota(jnp.int32, (beams, 2 * dishes), 1) < dishes
    zero_ref[0] = jnp.where(left, cosine, sine)
    zero_ref[1] = jnp.where(left, -sine, cosine)
    for table_ref, stride in ((fine_ref, 1), (coarse_ref, comb)):
        shift = (TWO_PI * BAND_WIDTH / chans * stride) * tau
        count = table_ref.shape[0]
        cosine, sine = small_phasor(shift)
        powers = [(jnp.ones_like(tau), jnp.zeros_like(tau)), (cosine, -sine)]
        for k in range(2, count):
            powers.append(cmul(powers[k // 2], powers[k - k // 2]))
        for k in range(count):
            table_ref[k, 0] = powers[k][0]
            table_ref[k, 1] = powers[k][1]

    for g in range(groups):
        if g % per == 0:
            volt_copy(g // per).wait()
        slot = g % rows_ref.shape[0]
        for i in range(group):
            ja, cb = i % part_rows, g * group_combs + i // part_rows
            if ja == 0:
                base = cmul((zero_ref[0], zero_ref[1]), (fine_ref[cb, 0], fine_ref[cb, 1]))
            weight = cmul(base, (coarse_ref[ja, 0], coarse_ref[ja, 1]))
            stacked = jnp.concatenate(weight, 0).astype(BF16)
            formed = jnp.dot(stacked, volt_ref[ja, cb], preferred_element_type=F32)
            rows_ref[slot, 0, pl.ds(i, beams, stride=group), :] = formed[:beams]
            rows_ref[slot, 1, pl.ds(i, beams, stride=group), :] = formed[beams:]
        rows = pl.ds(g * group, group)
        for p in range(2):
            out_ref[:, rows, p * samples : (p + 1) * samples] = (
                rows_ref[slot, p].reshape(beams, group, samples).astype(BF16)
            )
        if g % per == per - 1:
            out_copy(g // per).start()

    for g in range(chunks):
        out_copy(g).wait()


def form_beams(voltages, delays, pointing, dish_mask, chans, comb):
    chan_dev, _, dishes, samples = voltages.shape
    beams = pointing.shape[0]
    part_rows = chan_dev // comb
    group = part_rows * max(1, 16 // part_rows)
    chunks = math.gcd(2, chan_dev // group)
    hbm = pl.BlockSpec(memory_space=pltpu.HBM)
    volt = voltages.reshape(part_rows, comb, 2 * dishes, samples)
    return pl.pallas_call(
        functools.partial(beam_kernel, chans, comb),
        out_shape=jax.ShapeDtypeStruct((beams, chan_dev, 2 * samples), BF16),
        in_specs=[pl.BlockSpec(memory_space=pltpu.SMEM), hbm, hbm, hbm],
        out_specs=hbm,
        scratch_shapes=[
            pltpu.VMEM((dishes, delays.shape[0]), F32),
            pltpu.VMEM((1, dishes), jnp.int32),
            pltpu.VMEM(volt.shape, BF16),
            pltpu.VMEM((beams, chan_dev, 2 * samples), BF16),
            pltpu.VMEM((2, beams, 2 * dishes), F32),
            pltpu.VMEM((comb, 2, beams, 2 * dishes), F32),
            pltpu.VMEM((part_rows, 2, beams, 2 * dishes), F32),
            pltpu.VMEM((2, 2, beams * group, samples), F32),
            pltpu.SemaphoreType.DMA((2,)),
            pltpu.SemaphoreType.DMA((chunks,)),
            pltpu.SemaphoreType.DMA((chunks,)),
        ],
        compiler_params=pltpu.CompilerParams(vmem_limit_bytes=60 * 2**20),
        name="form_beams",
    )(pointing, delays.T, dish_mask.reshape(1, dishes), volt)


def phasor(phase, points):
    half = points // 2
    angle = (TWO_PI / points) * ((phase + half) % points - half).astype(F32)
    return jnp.stack([jnp.cos(angle), jnp.sin(angle)], 0)


def chirp_tables(rate, samples, chans):
    length = samples * chans
    low, comb = 2 * samples, chans // (2 * samples)
    f = jnp.arange(samples, dtype=jnp.int32)[None, :]
    shift = 2 * rate * f % chans
    shift_low, shift_high = shift % low, shift // low
    inverse = rate * (2 - rate * rate) % (2 * comb)
    m = jnp.arange(comb, dtype=jnp.int32)[:, None]
    unit = length // (2 * comb)
    c_a = jnp.arange(samples, dtype=jnp.int32)[:, None]
    turn_a = phasor(-(rate * c_a * f % samples), samples)
    turn_b = phasor(-(rate * m * f % (chans // 2)), chans // 2)
    quad = inverse * m * m % (2 * comb) * unit
    place = (m - shift_high) % comb
    wrap = jnp.where(place == 0, comb, 0)
    before = [phasor(quad - (place + beta * wrap) * low * f, length) for beta in range(2)]
    place = rate * m % comb
    quad = inverse * place * place % (2 * comb) * unit
    gauss_phase = -(rate * m * m % (2 * comb)) * unit
    gauss = jnp.sum(phasor(gauss_phase, length), axis=1)
    scale = 2 * samples / (length * math.sqrt(chans))
    turned = phasor(quad + low * place * f + f * shift_low - rate * f * f % length, length)
    after = cmul((turned[0], turned[1]), (gauss[0] * scale, gauss[1] * scale))
    return turn_a, turn_b, jnp.stack(before), jnp.stack(after), shift_low


def time_matrix(samples):
    t = jnp.arange(samples, dtype=jnp.int32)
    cosine, sine = phasor(t[:, None] * t[None, :] % samples, samples)
    return jnp.concatenate(
        [jnp.concatenate([cosine, -sine], 1), jnp.concatenate([sine, cosine], 1)], 0
    ).astype(BF16)


def mix_matrices(samples, chans):
    low, comb = 2 * samples, chans // (2 * samples)
    n = jnp.arange(low, dtype=jnp.int32)
    c_b = jnp.arange(comb, dtype=jnp.int32)
    product = (comb * n[None, None, :] + c_b[:, None, None]) * n[None, :, None] % chans
    cosine, sine = phasor(product, chans)
    both = jnp.stack([cosine.reshape(comb, low // 8, 8, low), sine.reshape(comb, low // 8, 8, low)], 2)
    return both.reshape(comb, 2 * low, low).astype(BF16)


def dedisperse_kernel(
    chans, rate_ref, beam_ref, time_ref, mix_hbm, turn_a_ref, turn_b_ref, before_ref, after_ref,
    shift_ref, out_hbm, grid_ref, power_ref, scaled_ref, mix_ref, out_ref, moved_ref, mix_sem, out_sem,
):
    samples = turn_a_ref.shape[1]
    low, comb = 2 * samples, grid_ref.shape[0]
    ahead = min(16, comb)

    def mix_copy(c):
        part = pl.ds(c * (comb // 2), comb // 2)
        return pltpu.make_async_copy(mix_hbm.at[part], mix_ref.at[part], mix_sem.at[c])

    def out_copy(high):
        lanes = pl.ds(high * low, low)
        return pltpu.make_async_copy(
            out_ref.at[:, :, lanes], out_hbm.at[0, :, :, lanes], out_sem.at[high]
        )

    for c in range(2):
        mix_copy(c).start()
    power_ref[...] = jnp.zeros_like(power_ref)

    for c_b in range(comb):
        beam = beam_ref[:, c_b].reshape(low, 2 * samples)
        wide = beam.astype(F32)
        power_ref[...] += jnp.sum((wide * wide).reshape(low // 8, 8, 2 * samples), 0)
        spectrum = jnp.dot(beam, time_ref[...], preferred_element_type=F32)
        turned = cmul(
            (turn_a_ref[0], turn_a_ref[1]),
            (turn_b_ref[0, pl.ds(c_b, 1), :], turn_b_ref[1, pl.ds(c_b, 1), :]),
        )
        halves = []
        for h in range(2):
            piece = spectrum[h * samples : (h + 1) * samples]
            moved = cmul((piece[:, :samples], piece[:, samples:]), turned)
            halves.append(jnp.concatenate(moved, 1).astype(BF16))
        moved_ref[c_b] = jnp.concatenate(halves, 0)

    for c_b in range(comb):
        moved = moved_ref[c_b]
        if c_b % (comb // 2) == 0:
            mix_copy(c_b // (comb // 2)).wait()


        mixed = jnp.dot(mix_ref[c_b], moved, preferred_element_type=F32)
        mixed = mixed.reshape(low // 8, 2, 8, 2 * samples)
        real = mixed[:, 0, :, :samples] - mixed[:, 1, :, samples:]
        imag = mixed[:, 0, :, samples:] + mixed[:, 1, :, :samples]
        grid_ref[c_b, 0] = real.reshape(low, samples)
        grid_ref[c_b, 1] = imag.reshape(low, samples)

    mean_power = jnp.sum(power_ref[...]) / (samples * chans)
    factor = lax.rsqrt(jnp.full((1, samples), mean_power, F32) + EPSILON)
    for p in range(2):
        scaled_ref[p] = after_ref[p] * factor
    rate = 2 * rate_ref[0] + 1

    @pl.loop(0, low // 8, unroll=1)
    def _(tile):
        rows = pl.ds(pl.multiple_of(tile * 8, 8), 8)
        values = [(grid_ref[c, 0, rows, :], grid_ref[c, 1, rows, :]) for c in range(comb)]
        values = fft_list(values, 1)
        position = tile * 8 + lax.broadcasted_iota(jnp.int32, (8, samples), 0)
        wrapped = position < shift_ref[...]
        for m in range(comb):
            table = [
                jnp.where(wrapped, before_ref[1, p, m : m + 1, :], before_ref[0, p, m : m + 1, :])
                for p in range(2)
            ]
            values[m] = cmul(values[m], table)
        values = fft_list(values, -1)
        for k in range(comb):
            real, imag = cmul(values[k], [scaled_ref[p, k : k + 1, :] for p in range(2)])
            place = lax.rem(rate * k, comb)
            grid_ref[place, 0, rows, :] = real
            grid_ref[place, 1, rows, :] = imag

    @pl.loop(0, comb, unroll=4)
    def _(high):
        both = jnp.concatenate([grid_ref[high, 0], grid_ref[high, 1]], 1).astype(BF16)
        result = lax.dot_general(
            time_ref[...], both, (((1,), (1,)), ((), ())), preferred_element_type=F32
        )
        lanes = pl.ds(pl.multiple_of(high * low, low), low)
        out_ref[0, :, lanes] = result[:samples]
        out_ref[1, :, lanes] = result[samples:]
        out_copy(high).start()

    @pl.loop(0, comb)
    def _(high):
        out_copy(high).wait()


def dedisperse(beam, trial, samples, chans):
    low, comb = 2 * samples, chans // (2 * samples)
    tables = chirp_tables(2 * trial[0] + 1, samples, chans)
    time_mat = time_matrix(samples)
    mix = mix_matrices(samples, chans)
    hbm = pl.BlockSpec(memory_space=pltpu.HBM)
    vmem = pl.BlockSpec(memory_space=pltpu.VMEM)
    return pl.pallas_call(
        functools.partial(dedisperse_kernel, chans),
        out_shape=jax.ShapeDtypeStruct((1, 2, samples, chans), F32),
        in_specs=[pl.BlockSpec(memory_space=pltpu.SMEM), vmem, vmem, hbm] + [vmem] * len(tables),
        out_specs=hbm,
        scratch_shapes=[
            pltpu.VMEM((comb, 2, low, samples), F32),
            pltpu.VMEM((8, 2 * samples), F32),
            pltpu.VMEM((2, comb, samples), F32),
            pltpu.VMEM(mix.shape, BF16),
            pltpu.VMEM((2, samples, chans), F32),
            pltpu.VMEM((comb, low, low), BF16),
            pltpu.SemaphoreType.DMA((comb,)),
            pltpu.SemaphoreType.DMA((comb,)),
        ],
        compiler_params=pltpu.CompilerParams(vmem_limit_bytes=50 * 2**20),
        name="dedisperse",
    )(trial, beam, time_mat, mix, *tables)


def on_device(chan_devs, voltages, delays, pointing, dm_index, dish_mask):
    chan_dev, _, _, samples = voltages.shape
    chans = chan_dev * chan_devs
    comb = chans // (2 * samples)
    beam_dev = dm_index.shape[0]
    formed = form_beams(voltages, delays, pointing, dish_mask, chans, comb)
    formed = lax.all_to_all(formed, "chan", split_axis=0, concat_axis=0, tiled=True)
    part_rows = chan_dev // comb
    formed = formed.reshape(chan_devs, beam_dev, comb, part_rows, 2 * samples)
    if part_rows % 16:
        formed = jnp.transpose(formed, (1, 2, 0, 3, 4)).reshape(
            1, beam_dev, comb, chans // comb, 2 * samples
        )
    pieces = [
        dedisperse(formed[:, b], dm_index[b : b + 1], samples, chans) for b in range(beam_dev)
    ]
    return pieces[0] if beam_dev == 1 else jnp.concatenate(pieces, 0)


def solution(mesh):
    return jax.shard_map(
        functools.partial(on_device, mesh.shape["chan"]),
        mesh=mesh,
        in_specs=(
            P(("grp", "chan"), None, None, None),
            P(),
            P("grp"),
            P(("grp", "chan")),
            P("grp"),
        ),
        out_specs=P(("grp", "chan"), None, None, None),
        check_vma=False,
    )
```

time: 77.9 us -> 69.8 us (0.90)
  Pallas kernels: 23.7 us -> 15.7 us
    pallas_call x1, Pallas kernels: 14 us -> 8.79 us  [dedisperse(): pl.pallas_call(functools.partial(dedisperse_kernel, chans), out_shape=jax...]
    pallas_call x1, Pallas kernels: 9.67 us -> 6.86 us  [form_beams(): pl.pallas_call(functools.partial(beam_kernel, chans, comb), out_shape=jax...]
    another operation x3 -> x4, other arithmetic: 20 us -> 22.8 us
    concatenate x1 -> x0, other arithmetic: 2.34 us -> none  [mix_matrices(): return jnp.concatenate([cosine, sine], 1).astype(BF16)]
  transfers between devices with their start and end apart: 1 -> 1, of which waited for: 1 -> 1; matrix products, arithmetic and copies ran while one was open for 31% -> 35% of each run, Pallas kernels for 0% -> 0%
where the time goes in v2:
time: 69.8 us; the launch traced here: 69.6 us
  other arithmetic  24 us (34%)
  waiting for transfers between devices  20.8 us (30%)
  Pallas kernels  15.7 us (22%)
  starting transfers between devices  6.57 us (9%)
  between operations  2.02 us (3%)
    all_to_all x1, waiting for transfers between devices, on_device(): lax.all_to_all(formed, 'chan', split_axis=0, concat_axis=0, tiled=True)  20.8 us
    another operation x3, other arithmetic  20.5 us
    pallas_call x1, Pallas kernels, dedisperse(): pl.pallas_call(functools.partial(dedisperse_kernel, chans), out_shape=jax...  8.79 us
    pallas_call x1, Pallas kernels, form_beams(): pl.pallas_call(functools.partial(beam_kernel, chans, comb), out_shape=jax...  6.86 us
    all_to_all x1, starting transfers between devices, on_device(): lax.all_to_all(formed, 'chan', split_axis=0, concat_axis=0, tiled=True)  6.57 us
    another operation x1, other arithmetic, mix_matrices(): jnp.stack([cosine.reshape(comb, low // 8, 8, low), sine.reshape(comb, low...  2.31 us
  transfers between devices with their start and end apart: 1, of which 1 were waited for; matrix products, arithmetic and copies ran while one was open for 35% of the time, Pallas kernels for 0%

profile of v2, /device:TPU:13, one launch (start us, length us, event | category | flops | bytes accessed | tf_op | source)
XLA Modules:
  0.0 69.6 jit_solution(5198761956057783682)
XLA Ops:
  0.0 6.9 %form_beams.1 = bf16[16,256,256]{2,1,0:T(8,128)(2,1)} custom-call(s32[16]{0:T(128)} %point_ref.1, f32[64,512]{1,0:T(8,128)} %bitcast.15, s32[1,64]{1,0:T(1,128)} %bitcast.16, bf16[16,16,128,128]{3,2,1,0:T(8,128)(2,1)} %bitcast.14), custom_call_target="tpu_custom_call" | custom-call | tf_op jit(solution)/shard_map/form_beams/pallas_call | solution.py:201
  6.9 6.6 %all-to-all-start = ((bf16[16,256,256]{2,1,0:T(8,128)(2,1)}), bf16[16,256,256]{2,1,0:T(8,128)(2,1)S(1)}, u32[]{:S(2)}, u32[]{:S(2)}) async-start(bf16[16,256,256]{2,1,0:T(8,128)(2,1)} %form_beams.1), calls=%async_computation | async-start | bytes 4194304 | tf_op jit(solution)/shard_map/all_to_all | solution.py:400
  14.1 0.1 fusion.81
  14.2 0.1 maximum_reduce_fusion
  14.3 0.6 fusion.83
  16.2 0.1 multiply_subtract_fusion
  16.4 0.1 fusion.62
  16.5 0.2 fusion.58
  16.7 0.3 fusion.28
  17.0 0.3 negate_convert_fusion
  17.4 0.4 fusion.26
  17.8 19.9 %cosine_convert_fusion = (bf16[16,32,1,8,256]{4,3,2,1,0:T(8,128)(2,1)S(1)}, bf16[16,32,1,8,256]{4,3,2,1,0:T(8,128)(2,1)S(1)}) fusion(s32[32,8]{1,0:T(8,128)S(1)} %multiply_add_fusion, s32[16,256]{1,0:T(8,128)S(1)} %iota_add_fusion), kind=kLoop, calls=%fused_computation.16 | loop fusion | flops 30408704 | bytes 4211712 | tf_op jit(solution)/shard_map/convert
  37.7 2.3 %pad_maximum_fusion = bf16[16,32,2,8,256]{4,3,2,1,0:T(8,128)(2,1)} fusion(bf16[16,32,1,8,256]{4,3,2,1,0:T(8,128)(2,1)S(1)} %get-tuple-element.6, bf16[16,32,1,8,256]{4,3,2,1,0:T(8,128)(2,1)S(1)} %get-tuple-element.5), kind=kLoop, calls=%fused_computation.14 | loop fusion | flops 2097152 | bytes 8388608 | tf_op jit(solution)/shard_map/stack | solution.py:270
  40.0 20.8 %all-to-all-done = bf16[16,256,256]{2,1,0:T(8,128)(2,1)S(1)} async-done(((bf16[16,256,256]{2,1,0:T(8,128)(2,1)}), bf16[16,256,256]{2,1,0:T(8,128)(2,1)S(1)}, u32[]{:S(2)}, u32[]{:S(2)}) %all-to-all-start) | async-done | bytes 2097184 | tf_op jit(solution)/shard_map/all_to_all | solution.py:400
  60.9 8.8 %dedisperse.1 = f32[1,2,128,4096]{3,2,1,0:T(8,128)} custom-call(s32[1]{0:T(128)S(6)} %copy.6.rate_ref, bf16[16,16,16,256]{3,2,1,0:T(8,128)(2,1)S(1)} %bitcast.12, bf16[256,256]{1,0:T(8,128)(2,1)S(1)} %maximum_maximum_fusion.time_ref, bf16[16,512,256]{2,1,0:T(8,128)(2,1)} %bitcast.13, f32[2,128,128]{2,1,0:T(8,128)S(1)} %pad_maximum_fusion.1.turn_a_ref, ...), custom_call_target="tpu_custom_call" | custom-call | tf_op jit(solution)/shard_map/dedisperse/pallas_call | solution.py:374
  (17 shorter events, 0.2 us)
Async XLA Ops:
  6.9 54.0 %all-to-all-start = ((bf16[16,256,256]{2,1,0:T(8,128)(2,1)}), bf16[16,256,256]{2,1,0:T(8,128)(2,1)S(1)}, u32[]{:S(2)}, u32[]{:S(2)}) async-start(bf16[16,256,256]{2,1,0:T(8,128)(2,1)} %form_beams.1), calls=%async_computation | async-start | bytes 4194304 | tf_op jit(solution)/shard_map/all_to_all | solution.py:400

commit v3 on v2

--- a/solution.py
+++ b/solution.py
@@ -105,24 +105,26 @@
     group_combs = group // part_rows
     groups = chan_dev // group
     chunks = volt_sem.shape[0]
-    per = groups // chunks
+    ends = [groups * end // 16 for end in (6, 11, 14, 16)] if chunks > 1 else [groups]
+    begins = [0] + ends[:-1]
 
     def volt_copy(g):
-        combs = pl.ds(g * per * group_combs, per * group_combs)
+        combs = pl.ds(begins[g] * group_combs, (ends[g] - begins[g]) * group_combs)
         return pltpu.make_async_copy(volt_hbm.at[:, combs], volt_ref.at[:, combs], volt_sem.at[g])
 
     def out_copy(g):
-        rows = pl.ds(g * per * group, per * group)
+        rows = pl.ds(begins[g] * group, (ends[g] - begins[g]) * group)
         return pltpu.make_async_copy(out_ref.at[:, rows], out_hbm.at[:, rows], out_sem.at[g])
 
     delay_copy = pltpu.make_async_copy(delay_hbm, delay_ref, small_sem.at[0])
     mask_copy = pltpu.make_async_copy(mask_hbm, mask_ref, small_sem.at[1])
     delay_copy.start()
     mask_copy.start()
-    for g in range(chunks):
-        volt_copy(g).start()
+    volt_copy(0).start()
     delay_copy.wait()
     mask_copy.wait()
+    if chunks > 1:
+        volt_copy(1).start()
 
     table_rows = delay_ref.shape[1]
     place = lax.broadcasted_iota(jnp.int32, (beams, table_rows), 1)
@@ -166,25 +168,38 @@
             table_ref[k, 1] = powers[k][1]
 
     for g in range(groups):
-        if g % per == 0:
-            volt_copy(g // per).wait()
+        if g in begins:
+            chunk = begins.index(g)
+            volt_copy(chunk).wait()
+            if chunk + 2 < chunks:
+                volt_copy(chunk + 2).start()
         slot = g % rows_ref.shape[0]
-        for i in range(group):
-            ja, cb = i % part_rows, g * group_combs + i // part_rows
-            if ja == 0:
-                base = cmul((zero_ref[0], zero_ref[1]), (fine_ref[cb, 0], fine_ref[cb, 1]))
-            weight = cmul(base, (coarse_ref[ja, 0], coarse_ref[ja, 1]))
-            stacked = jnp.concatenate(weight, 0).astype(BF16)
-            formed = jnp.dot(stacked, volt_ref[ja, cb], preferred_element_type=F32)
-            rows_ref[slot, 0, pl.ds(i, beams, stride=group), :] = formed[:beams]
-            rows_ref[slot, 1, pl.ds(i, beams, stride=group), :] = formed[beams:]
+        for i in range(0, group, 2):
+            weights, sources = [], []
+            for k in range(i, i + 2):
+                ja, cb = k % part_rows, g * group_combs + k // part_rows
+                if ja == 0:
+                    base = cmul((zero_ref[0], zero_ref[1]), (fine_ref[cb, 0], fine_ref[cb, 1]))
+                weight = cmul(base, (coarse_ref[ja, 0], coarse_ref[ja, 1]))
+                weights.append(jnp.concatenate(weight, 0).astype(BF16))
+                sources.append(volt_ref[ja, cb])
+            blank = jnp.zeros_like(weights[0])
+            stacked = jnp.concatenate(
+                [jnp.concatenate([weights[0], blank], 1), jnp.concatenate([blank, weights[1]], 1)], 0
+            )
+            formed = jnp.dot(stacked, jnp.concatenate(sources, 0), preferred_element_type=F32)
+            for k in range(2):
+                for p in range(2):
+                    rows_ref[slot, p, pl.ds(i + k, beams, stride=group), :] = formed[
+                        (2 * k + p) * beams : (2 * k + p + 1) * beams
+                    ]
         rows = pl.ds(g * group, group)
         for p in range(2):
             out_ref[:, rows, p * samples : (p + 1) * samples] = (
                 rows_ref[slot, p].reshape(beams, group, samples).astype(BF16)
             )
-        if g % per == per - 1:
-            out_copy(g // per).start()
+        if g + 1 in ends:
+            out_copy(chunk).start()
 
     for g in range(chunks):
         out_copy(g).wait()
@@ -195,7 +210,7 @@
     beams = pointing.shape[0]
     part_rows = chan_dev // comb
     group = part_rows * max(1, 16 // part_rows)
-    chunks = math.gcd(2, chan_dev // group)
+    chunks = 4 if (chan_dev // group) % 16 == 0 else 1
     hbm = pl.BlockSpec(memory_space=pltpu.HBM)
     volt = voltages.reshape(part_rows, comb, 2 * dishes, samples)
     return pl.pallas_call(
@@ -277,16 +292,15 @@
 ):
     samples = turn_a_ref.shape[1]
     low, comb = 2 * samples, grid_ref.shape[0]
-    ahead = min(16, comb)
 
     def mix_copy(c):
         part = pl.ds(c * (comb // 2), comb // 2)
         return pltpu.make_async_copy(mix_hbm.at[part], mix_ref.at[part], mix_sem.at[c])
 
-    def out_copy(high):
-        lanes = pl.ds(high * low, low)
+    def out_copy(half, high):
+        lanes = pl.ds(high * low + half * samples, samples)
         return pltpu.make_async_copy(
-            out_ref.at[:, :, lanes], out_hbm.at[0, :, :, lanes], out_sem.at[high]
+            out_ref.at[:, :, lanes], out_hbm.at[0, :, :, lanes], out_sem.at[half, high]
         )
 
     for c in range(2):
@@ -314,7 +328,6 @@
         if c_b % (comb // 2) == 0:
             mix_copy(c_b // (comb // 2)).wait()
 
-
         mixed = jnp.dot(mix_ref[c_b], moved, preferred_element_type=F32)
         mixed = mixed.reshape(low // 8, 2, 8, 2 * samples)
         real = mixed[:, 0, :, :samples] - mixed[:, 1, :, samples:]
@@ -328,8 +341,7 @@
         scaled_ref[p] = after_ref[p] * factor
     rate = 2 * rate_ref[0] + 1
 
-    @pl.loop(0, low // 8, unroll=1)
-    def _(tile):
+    def spread(tile):
         rows = pl.ds(pl.multiple_of(tile * 8, 8), 8)
         values = [(grid_ref[c, 0, rows, :], grid_ref[c, 1, rows, :]) for c in range(comb)]
         values = fft_list(values, 1)
@@ -348,20 +360,42 @@
             grid_ref[place, 0, rows, :] = real
             grid_ref[place, 1, rows, :] = imag
 
-    @pl.loop(0, comb, unroll=4)
-    def _(high):
-        both = jnp.concatenate([grid_ref[high, 0], grid_ref[high, 1]], 1).astype(BF16)
+    def finish(half, high):
+        rows = pl.ds(half * samples, samples)
+        both = [
+            jnp.concatenate([grid_ref[high + i, 0, rows], grid_ref[high + i, 1, rows]], 1)
+            for i in range(2)
+        ]
         result = lax.dot_general(
-            time_ref[...], both, (((1,), (1,)), ((), ())), preferred_element_type=F32
+            time_ref[...],
+            jnp.concatenate(both, 0).astype(BF16),
+            (((1,), (1,)), ((), ())),
+            preferred_element_type=F32,
         )
-        lanes = pl.ds(pl.multiple_of(high * low, low), low)
-        out_ref[0, :, lanes] = result[:samples]
-        out_ref[1, :, lanes] = result[samples:]
-        out_copy(high).start()
-
-    @pl.loop(0, comb)
-    def _(high):
-        out_copy(high).wait()
+        for i in range(2):
+            lanes = pl.ds((high + i) * low + half * samples, samples)
+            piece = result[:, i * samples : (i + 1) * samples]
+            out_ref[0, :, lanes] = piece[:samples]
+            out_ref[1, :, lanes] = piece[samples:]
+
+    tiles = samples // 8
+    for half in range(2):
+
+        @pl.loop(0, tiles, unroll=1)
+        def _(tile):
+            spread(half * tiles + tile)
+
+        for first in range(0, comb, 4):
+            for high in range(first, first + 4, 2):
+                finish(half, high)
+            for high in range(first, first + 4):
+                out_copy(half, high).start()
+
+    for half in range(2):
+
+        @pl.loop(0, comb)
+        def _(high):
+            out_copy(half, high).wait()
 
 
 def dedisperse(beam, trial, samples, chans):
@@ -383,8 +417,8 @@
             pltpu.VMEM(mix.shape, BF16),
             pltpu.VMEM((2, samples, chans), F32),
             pltpu.VMEM((comb, low, low), BF16),
-            pltpu.SemaphoreType.DMA((comb,)),
-            pltpu.SemaphoreType.DMA((comb,)),
+            pltpu.SemaphoreType.DMA((2,)),
+            pltpu.SemaphoreType.DMA((2, comb)),
         ],
         compiler_params=pltpu.CompilerParams(vmem_limit_bytes=50 * 2**20),
         name="dedisperse",

time: 69.8 us -> 69.2 us (level)
  Pallas kernels: 15.7 us -> 15 us
  transfers between devices with their start and end apart: 1 -> 1, of which waited for: 1 -> 1; matrix products, arithmetic and copies ran while one was open for 35% -> 36% of each run, Pallas kernels for 0% -> 0%
where the time goes in v3:
time: 69.2 us; the launch traced here: 69 us
  other arithmetic  24 us (35%)
  waiting for transfers between devices  20.8 us (30%)
  Pallas kernels  15 us (22%)
  starting transfers between devices  6.57 us (9%)
  between operations  2.02 us (3%)
    all_to_all x1, waiting for transfers between devices, on_device(): lax.all_to_all(formed, 'chan', split_axis=0, concat_axis=0, tiled=True)  20.8 us
    another operation x3, other arithmetic  20.5 us
    pallas_call x1, Pallas kernels, dedisperse(): pl.pallas_call(functools.partial(dedisperse_kernel, chans), out_shape=jax...  8.53 us
    all_to_all x1, starting transfers between devices, on_device(): lax.all_to_all(formed, 'chan', split_axis=0, concat_axis=0, tiled=True)  6.57 us
    pallas_call x1, Pallas kernels, form_beams(): pl.pallas_call(functools.partial(beam_kernel, chans, comb), out_shape=jax...  6.45 us
    another operation x1, other arithmetic, mix_matrices(): jnp.stack([cosine.reshape(comb, low // 8, 8, low), sine.reshape(comb, low...  2.31 us
  transfers between devices with their start and end apart: 1, of which 1 were waited for; matrix products, arithmetic and copies ran while one was open for 36% of the time, Pallas kernels for 0%

profile of v3, /device:TPU:13, one launch (start us, length us, event | category | flops | bytes accessed | tf_op | source)
XLA Modules:
  0.0 69.0 jit_solution(8778113471466600006)
XLA Ops:
  0.0 6.5 %form_beams.1 = bf16[16,256,256]{2,1,0:T(8,128)(2,1)} custom-call(s32[16]{0:T(128)} %point_ref.1, f32[64,512]{1,0:T(8,128)} %bitcast.15, s32[1,64]{1,0:T(1,128)} %bitcast.16, bf16[16,16,128,128]{3,2,1,0:T(8,128)(2,1)} %bitcast.14), custom_call_target="tpu_custom_call" | custom-call | tf_op jit(solution)/shard_map/form_beams/pallas_call | solution.py:216
  6.5 6.6 %all-to-all-start = ((bf16[16,256,256]{2,1,0:T(8,128)(2,1)}), bf16[16,256,256]{2,1,0:T(8,128)(2,1)S(1)}, u32[]{:S(2)}, u32[]{:S(2)}) async-start(bf16[16,256,256]{2,1,0:T(8,128)(2,1)} %form_beams.1), calls=%async_computation | async-start | bytes 4194304 | tf_op jit(solution)/shard_map/all_to_all | solution.py:434
  13.7 0.1 fusion.81
  13.8 0.1 maximum_reduce_fusion
  13.9 0.6 fusion.83
  15.8 0.1 multiply_subtract_fusion
  16.0 0.1 fusion.62
  16.1 0.2 fusion.58
  16.3 0.3 fusion.28
  16.6 0.3 negate_convert_fusion
  17.0 0.4 fusion.26
  17.4 19.9 %cosine_convert_fusion = (bf16[16,32,1,8,256]{4,3,2,1,0:T(8,128)(2,1)S(1)}, bf16[16,32,1,8,256]{4,3,2,1,0:T(8,128)(2,1)S(1)}) fusion(s32[32,8]{1,0:T(8,128)S(1)} %multiply_add_fusion, s32[16,256]{1,0:T(8,128)S(1)} %iota_add_fusion), kind=kLoop, calls=%fused_computation.16 | loop fusion | flops 30408704 | bytes 4211712 | tf_op jit(solution)/shard_map/convert
  37.3 2.3 %pad_maximum_fusion = bf16[16,32,2,8,256]{4,3,2,1,0:T(8,128)(2,1)} fusion(bf16[16,32,1,8,256]{4,3,2,1,0:T(8,128)(2,1)S(1)} %get-tuple-element.6, bf16[16,32,1,8,256]{4,3,2,1,0:T(8,128)(2,1)S(1)} %get-tuple-element.5), kind=kLoop, calls=%fused_computation.14 | loop fusion | flops 2097152 | bytes 8388608 | tf_op jit(solution)/shard_map/stack | solution.py:285
  39.6 20.8 %all-to-all-done = bf16[16,256,256]{2,1,0:T(8,128)(2,1)S(1)} async-done(((bf16[16,256,256]{2,1,0:T(8,128)(2,1)}), bf16[16,256,256]{2,1,0:T(8,128)(2,1)S(1)}, u32[]{:S(2)}, u32[]{:S(2)}) %all-to-all-start) | async-done | bytes 2097184 | tf_op jit(solution)/shard_map/all_to_all | solution.py:434
  60.4 8.5 %dedisperse.1 = f32[1,2,128,4096]{3,2,1,0:T(8,128)} custom-call(s32[1]{0:T(128)S(6)} %copy.6.rate_ref, bf16[16,16,16,256]{3,2,1,0:T(8,128)(2,1)S(1)} %bitcast.12, bf16[256,256]{1,0:T(8,128)(2,1)S(1)} %maximum_maximum_fusion.time_ref, bf16[16,512,256]{2,1,0:T(8,128)(2,1)} %bitcast.13, f32[2,128,128]{2,1,0:T(8,128)S(1)} %pad_maximum_fusion.1.turn_a_ref, ...), custom_call_target="tpu_custom_call" | custom-call | tf_op jit(solution)/shard_map/dedisperse/pallas_call | solution.py:408
  (17 shorter events, 0.2 us)
Async XLA Ops:
  6.5 54.0 %all-to-all-start = ((bf16[16,256,256]{2,1,0:T(8,128)(2,1)}), bf16[16,256,256]{2,1,0:T(8,128)(2,1)S(1)}, u32[]{:S(2)}, u32[]{:S(2)}) async-start(bf16[16,256,256]{2,1,0:T(8,128)(2,1)} %form_beams.1), calls=%async_computation | async-start | bytes 4194304 | tf_op jit(solution)/shard_map/all_to_all | solution.py:434

commit v4 on v3

--- a/solution.py
+++ b/solution.py
@@ -276,26 +276,27 @@
     ).astype(BF16)
 
 
-def mix_matrices(samples, chans):
+def mix_matrix(samples):
+    low = 2 * samples
+    n = jnp.arange(low, dtype=jnp.int32)
+    cosine, sine = phasor(n[None, :] * n[:, None] % low, low)
+    both = jnp.stack([cosine.reshape(low // 8, 8, low), sine.reshape(low // 8, 8, low)], 1)
+    return both.reshape(2 * low, low).astype(BF16)
+
+
+def comb_twiddles(samples, chans):
     low, comb = 2 * samples, chans // (2 * samples)
-    n = jnp.arange(low, dtype=jnp.int32)
-    c_b = jnp.arange(comb, dtype=jnp.int32)
-    product = (comb * n[None, None, :] + c_b[:, None, None]) * n[None, :, None] % chans
-    cosine, sine = phasor(product, chans)
-    both = jnp.stack([cosine.reshape(comb, low // 8, 8, low), sine.reshape(comb, low // 8, 8, low)], 2)
-    return both.reshape(comb, 2 * low, low).astype(BF16)
+    n = jnp.arange(low, dtype=jnp.int32)[:, None]
+    c_b = jnp.arange(comb, dtype=jnp.int32)[None, :]
+    return phasor(n * c_b % chans, chans)
 
 
 def dedisperse_kernel(
-    chans, rate_ref, beam_ref, time_ref, mix_hbm, turn_a_ref, turn_b_ref, before_ref, after_ref,
-    shift_ref, out_hbm, grid_ref, power_ref, scaled_ref, mix_ref, out_ref, moved_ref, mix_sem, out_sem,
+    chans, rate_ref, beam_ref, time_ref, mix_ref, twiddle_ref, turn_a_ref, turn_b_ref, before_ref, after_ref,
+    shift_ref, out_hbm, grid_ref, power_ref, scaled_ref, out_ref, moved_ref, out_sem,
 ):
     samples = turn_a_ref.shape[1]
     low, comb = 2 * samples, grid_ref.shape[0]
-
-    def mix_copy(c):
-        part = pl.ds(c * (comb // 2), comb // 2)
-        return pltpu.make_async_copy(mix_hbm.at[part], mix_ref.at[part], mix_sem.at[c])
 
     def out_copy(half, high):
         lanes = pl.ds(high * low + half * samples, samples)
@@ -303,8 +304,6 @@
             out_ref.at[:, :, lanes], out_hbm.at[0, :, :, lanes], out_sem.at[half, high]
         )
 
-    for c in range(2):
-        mix_copy(c).start()
     power_ref[...] = jnp.zeros_like(power_ref)
 
     for c_b in range(comb):
@@ -325,15 +324,15 @@
 
     for c_b in range(comb):
         moved = moved_ref[c_b]
-        if c_b % (comb // 2) == 0:
-            mix_copy(c_b // (comb // 2)).wait()
-
-        mixed = jnp.dot(mix_ref[c_b], moved, preferred_element_type=F32)
+
+        mixed = jnp.dot(mix_ref[...], moved, preferred_element_type=F32)
         mixed = mixed.reshape(low // 8, 2, 8, 2 * samples)
         real = mixed[:, 0, :, :samples] - mixed[:, 1, :, samples:]
         imag = mixed[:, 0, :, samples:] + mixed[:, 1, :, :samples]
-        grid_ref[c_b, 0] = real.reshape(low, samples)
-        grid_ref[c_b, 1] = imag.reshape(low, samples)
+        values = (real.reshape(low, samples), imag.reshape(low, samples))
+        if c_b:
+            values = cmul(values, [twiddle_ref[p, :, c_b : c_b + 1] for p in range(2)])
+        grid_ref[c_b, 0], grid_ref[c_b, 1] = values
 
     mean_power = jnp.sum(power_ref[...]) / (samples * chans)
     factor = lax.rsqrt(jnp.full((1, samples), mean_power, F32) + EPSILON)
@@ -402,27 +401,25 @@
     low, comb = 2 * samples, chans // (2 * samples)
     tables = chirp_tables(2 * trial[0] + 1, samples, chans)
     time_mat = time_matrix(samples)
-    mix = mix_matrices(samples, chans)
+    mix, twiddles = mix_matrix(samples), comb_twiddles(samples, chans)
     hbm = pl.BlockSpec(memory_space=pltpu.HBM)
     vmem = pl.BlockSpec(memory_space=pltpu.VMEM)
     return pl.pallas_call(
         functools.partial(dedisperse_kernel, chans),
         out_shape=jax.ShapeDtypeStruct((1, 2, samples, chans), F32),
-        in_specs=[pl.BlockSpec(memory_space=pltpu.SMEM), vmem, vmem, hbm] + [vmem] * len(tables),
+        in_specs=[pl.BlockSpec(memory_space=pltpu.SMEM), vmem, vmem, vmem, vmem] + [vmem] * len(tables),
         out_specs=hbm,
         scratch_shapes=[
             pltpu.VMEM((comb, 2, low, samples), F32),
             pltpu.VMEM((8, 2 * samples), F32),
             pltpu.VMEM((2, comb, samples), F32),
-            pltpu.VMEM(mix.shape, BF16),
             pltpu.VMEM((2, samples, chans), F32),
             pltpu.VMEM((comb, low, low), BF16),
-            pltpu.SemaphoreType.DMA((2,)),
             pltpu.SemaphoreType.DMA((2, comb)),
         ],
         compiler_params=pltpu.CompilerParams(vmem_limit_bytes=50 * 2**20),
         name="dedisperse",
-    )(trial, beam, time_mat, mix, *tables)
+    )(trial, beam, time_mat, mix, twiddles, *tables)
 
 
 def on_device(chan_devs, voltages, delays, pointing, dm_index, dish_mask):

time: 69.2 us -> 68.9 us (level)
  other arithmetic: 24 us -> 3.27 us
  waiting for transfers between devices: 20.8 us -> 41.4 us
    another operation x4, other arithmetic: 22.8 us -> 2.03 us
    all_to_all x1, waiting for transfers between devices: 20.8 us -> 41.4 us  [on_device(): lax.all_to_all(formed, 'chan', split_axis=0, concat_axis=0, tiled=True)]
  transfers between devices with their start and end apart: 1 -> 1, of which waited for: 1 -> 1; matrix products, arithmetic and copies ran while one was open for 36% -> 6% of each run, Pallas kernels for 0% -> 0%
where the time goes in v4:
time: 68.9 us; the launch traced here: 68.7 us
  waiting for transfers between devices  41.4 us (60%)
  Pallas kernels  14.7 us (21%)
  starting transfers between devices  6.57 us (10%)
  other arithmetic  3.27 us (5%)
  between operations  2.03 us (3%)
  local copies, waits for them, and re-layouts  0.75 us (1%)
    all_to_all x1, waiting for transfers between devices, on_device(): lax.all_to_all(formed, 'chan', split_axis=0, concat_axis=0, tiled=True)  41.4 us
    pallas_call x1, Pallas kernels, dedisperse(): pl.pallas_call(functools.partial(dedisperse_kernel, chans), out_shape=jax...  8.21 us
    all_to_all x1, starting transfers between devices, on_device(): lax.all_to_all(formed, 'chan', split_axis=0, concat_axis=0, tiled=True)  6.57 us
    pallas_call x1, Pallas kernels, form_beams(): pl.pallas_call(functools.partial(beam_kernel, chans, comb), out_shape=jax...  6.45 us
    another operation x3, other arithmetic  2 us
  transfers between devices with their start and end apart: 1, of which 1 were waited for; matrix products, arithmetic and copies ran while one was open for 6% of the time, Pallas kernels for 0%

profile of v4, /device:TPU:13, one launch (start us, length us, event | category | flops | bytes accessed | tf_op | source)
XLA Modules:
  0.0 68.7 jit_solution(3776495377094738573)
XLA Ops:
  0.0 6.5 %form_beams.1 = bf16[16,256,256]{2,1,0:T(8,128)(2,1)} custom-call(s32[16]{0:T(128)} %point_ref.1, f32[64,512]{1,0:T(8,128)} %bitcast.15, s32[1,64]{1,0:T(1,128)} %bitcast.16, bf16[16,16,128,128]{3,2,1,0:T(8,128)(2,1)} %bitcast.14), custom_call_target="tpu_custom_call" | custom-call | tf_op jit(solution)/shard_map/form_beams/pallas_call | solution.py:216
  6.5 6.6 %all-to-all-start = ((bf16[16,256,256]{2,1,0:T(8,128)(2,1)}), bf16[16,256,256]{2,1,0:T(8,128)(2,1)S(1)}, u32[]{:S(2)}, u32[]{:S(2)}) async-start(bf16[16,256,256]{2,1,0:T(8,128)(2,1)} %form_beams.1), calls=%async_computation | async-start | bytes 4194304 | tf_op jit(solution)/shard_map/all_to_all | solution.py:431
  13.7 0.1 fusion.95
  13.8 0.1 maximum_reduce_fusion
  13.9 0.6 fusion.97
  15.7 0.1 fusion.65
  15.8 0.1 copy.6.twiddle_ref
  16.1 0.1 multiply_subtract_fusion
  16.3 0.1 fusion.76
  16.4 0.2 fusion.72
  16.6 0.3 fusion.31
  16.9 0.3 negate_convert_fusion
  17.2 0.4 fusion.29
  17.6 1.4 %cosine_convert_fusion = (bf16[32,1,8,256]{3,2,1,0:T(8,128)(2,1)S(1)}, bf16[32,1,8,256]{3,2,1,0:T(8,128)(2,1)S(1)}) fusion(s32[32,8]{1,0:T(8,128)S(1)} %multiply_add_fusion), kind=kLoop, calls=%fused_computation.14 | loop fusion | flops 1900544 | bytes 263168 | tf_op jit(solution)/shard_map/convert
  19.1 41.4 %all-to-all-done = bf16[16,256,256]{2,1,0:T(8,128)(2,1)S(1)} async-done(((bf16[16,256,256]{2,1,0:T(8,128)(2,1)}), bf16[16,256,256]{2,1,0:T(8,128)(2,1)S(1)}, u32[]{:S(2)}, u32[]{:S(2)}) %all-to-all-start) | async-done | bytes 2097184 | tf_op jit(solution)/shard_map/all_to_all | solution.py:431
  60.4 8.2 %dedisperse.1 = f32[1,2,128,4096]{3,2,1,0:T(8,128)} custom-call(s32[1]{0:T(128)S(6)} %copy.7.rate_ref, bf16[16,16,16,256]{3,2,1,0:T(8,128)(2,1)S(1)} %bitcast.12, bf16[256,256]{1,0:T(8,128)(2,1)S(1)} %maximum_maximum_fusion.time_ref, bf16[512,256]{1,0:T(8,128)(2,1)S(1)} %bitcast.13, f32[2,256,16]{2,1,0:T(8,128)S(1)} %copy.6.twiddle_ref, ...), custom_call_target="tpu_custom_call" | custom-call | tf_op jit(solution)/shard_map/dedisperse/pallas_call | solution.py:407
  (17 shorter events, 0.2 us)
Async XLA Ops:
  6.5 54.0 %all-to-all-start = ((bf16[16,256,256]{2,1,0:T(8,128)(2,1)}), bf16[16,256,256]{2,1,0:T(8,128)(2,1)S(1)}, u32[]{:S(2)}, u32[]{:S(2)}) async-start(bf16[16,256,256]{2,1,0:T(8,128)(2,1)} %form_beams.1), calls=%async_computation | async-start | bytes 4194304 | tf_op jit(solution)/shard_map/all_to_all | solution.py:431

commit v5 on v4

--- a/solution.py
+++ b/solution.py
@@ -311,33 +311,34 @@
         wide = beam.astype(F32)
         power_ref[...] += jnp.sum((wide * wide).reshape(low // 8, 8, 2 * samples), 0)
         spectrum = jnp.dot(beam, time_ref[...], preferred_element_type=F32)
-        turned = cmul(
-            (turn_a_ref[0], turn_a_ref[1]),
-            (turn_b_ref[0, pl.ds(c_b, 1), :], turn_b_ref[1, pl.ds(c_b, 1), :]),
-        )
+        comb_turn = (turn_b_ref[0, pl.ds(c_b, 1), :], turn_b_ref[1, pl.ds(c_b, 1), :])
         halves = []
         for h in range(2):
             piece = spectrum[h * samples : (h + 1) * samples]
-            moved = cmul((piece[:, :samples], piece[:, samples:]), turned)
+            moved = cmul((piece[:, :samples], piece[:, samples:]), (turn_a_ref[0], turn_a_ref[1]))
+            moved = cmul(moved, comb_turn)
             halves.append(jnp.concatenate(moved, 1).astype(BF16))
         moved_ref[c_b] = jnp.concatenate(halves, 0)
-
-    for c_b in range(comb):
-        moved = moved_ref[c_b]
-
-        mixed = jnp.dot(mix_ref[...], moved, preferred_element_type=F32)
-        mixed = mixed.reshape(low // 8, 2, 8, 2 * samples)
-        real = mixed[:, 0, :, :samples] - mixed[:, 1, :, samples:]
-        imag = mixed[:, 0, :, samples:] + mixed[:, 1, :, :samples]
-        values = (real.reshape(low, samples), imag.reshape(low, samples))
-        if c_b:
-            values = cmul(values, [twiddle_ref[p, :, c_b : c_b + 1] for p in range(2)])
-        grid_ref[c_b, 0], grid_ref[c_b, 1] = values
 
     mean_power = jnp.sum(power_ref[...]) / (samples * chans)
     factor = lax.rsqrt(jnp.full((1, samples), mean_power, F32) + EPSILON)
     for p in range(2):
         scaled_ref[p] = after_ref[p] * factor
+    for c_b in range(comb):
+        moved = moved_ref[c_b]
+
+        mixed = jnp.dot(mix_ref[...], moved, preferred_element_type=F32)
+        for i in range(low // 8):
+            rows = pl.ds(8 * i, 8)
+            by_re, by_im = mixed[16 * i : 16 * i + 8], mixed[16 * i + 8 : 16 * i + 16]
+            values = (
+                by_re[:, :samples] - by_im[:, samples:],
+                by_re[:, samples:] + by_im[:, :samples],
+            )
+            if c_b:
+                values = cmul(values, [twiddle_ref[p, rows, c_b : c_b + 1] for p in range(2)])
+            grid_ref[c_b, 0, rows], grid_ref[c_b, 1, rows] = values
+
     rate = 2 * rate_ref[0] + 1
 
     def spread(tile):

time: 68.9 us -> 68.7 us (level)
  no operation moved by 1% of the time
where the time goes in v5:
time: 68.7 us; the launch traced here: 68.4 us
  waiting for transfers between devices  41.4 us (60%)
  Pallas kernels  14.4 us (21%)
  starting transfers between devices  6.57 us (10%)
  other arithmetic  3.27 us (5%)
  between operations  2.03 us (3%)
  local copies, waits for them, and re-layouts  0.75 us (1%)
    all_to_all x1, waiting for transfers between devices, on_device(): lax.all_to_all(formed, 'chan', split_axis=0, concat_axis=0, tiled=True)  41.4 us
    pallas_call x1, Pallas kernels, dedisperse(): pl.pallas_call(functools.partial(dedisperse_kernel, chans), out_shape=jax...  7.97 us
    all_to_all x1, starting transfers between devices, on_device(): lax.all_to_all(formed, 'chan', split_axis=0, concat_axis=0, tiled=True)  6.57 us
    pallas_call x1, Pallas kernels, form_beams(): pl.pallas_call(functools.partial(beam_kernel, chans, comb), out_shape=jax...  6.45 us
    another operation x3, other arithmetic  2 us
  transfers between devices with their start and end apart: 1, of which 1 were waited for; matrix products, arithmetic and copies ran while one was open for 6% of the time, Pallas kernels for 0%

profile of v5, /device:TPU:13, one launch (start us, length us, event | category | flops | bytes accessed | tf_op | source)
XLA Modules:
  0.0 68.4 jit_solution(2827654812008559332)
XLA Ops:
  0.0 6.5 %form_beams.1 = bf16[16,256,256]{2,1,0:T(8,128)(2,1)} custom-call(s32[16]{0:T(128)} %point_ref.1, f32[64,512]{1,0:T(8,128)} %bitcast.15, s32[1,64]{1,0:T(1,128)} %bitcast.16, bf16[16,16,128,128]{3,2,1,0:T(8,128)(2,1)} %bitcast.14), custom_call_target="tpu_custom_call" | custom-call | tf_op jit(solution)/shard_map/form_beams/pallas_call | solution.py:216
  6.5 6.6 %all-to-all-start = ((bf16[16,256,256]{2,1,0:T(8,128)(2,1)}), bf16[16,256,256]{2,1,0:T(8,128)(2,1)S(1)}, u32[]{:S(2)}, u32[]{:S(2)}) async-start(bf16[16,256,256]{2,1,0:T(8,128)(2,1)} %form_beams.1), calls=%async_computation | async-start | bytes 4194304 | tf_op jit(solution)/shard_map/all_to_all | solution.py:432
  13.7 0.1 fusion.95
  13.8 0.1 maximum_reduce_fusion
  13.9 0.6 fusion.97
  15.7 0.1 fusion.65
  15.8 0.1 copy.6.twiddle_ref
  16.1 0.1 multiply_subtract_fusion
  16.3 0.1 fusion.76
  16.4 0.2 fusion.72
  16.6 0.3 fusion.31
  16.9 0.3 negate_convert_fusion
  17.2 0.4 fusion.29
  17.6 1.4 %cosine_convert_fusion = (bf16[32,1,8,256]{3,2,1,0:T(8,128)(2,1)S(1)}, bf16[32,1,8,256]{3,2,1,0:T(8,128)(2,1)S(1)}) fusion(s32[32,8]{1,0:T(8,128)S(1)} %multiply_add_fusion), kind=kLoop, calls=%fused_computation.14 | loop fusion | flops 1900544 | bytes 263168 | tf_op jit(solution)/shard_map/convert
  19.1 41.4 %all-to-all-done = bf16[16,256,256]{2,1,0:T(8,128)(2,1)S(1)} async-done(((bf16[16,256,256]{2,1,0:T(8,128)(2,1)}), bf16[16,256,256]{2,1,0:T(8,128)(2,1)S(1)}, u32[]{:S(2)}, u32[]{:S(2)}) %all-to-all-start) | async-done | bytes 2097184 | tf_op jit(solution)/shard_map/all_to_all | solution.py:432
  60.4 8.0 %dedisperse.1 = f32[1,2,128,4096]{3,2,1,0:T(8,128)} custom-call(s32[1]{0:T(128)S(6)} %copy.7.rate_ref, bf16[16,16,16,256]{3,2,1,0:T(8,128)(2,1)S(1)} %bitcast.12, bf16[256,256]{1,0:T(8,128)(2,1)S(1)} %maximum_maximum_fusion.time_ref, bf16[512,256]{1,0:T(8,128)(2,1)S(1)} %bitcast.13, f32[2,256,16]{2,1,0:T(8,128)S(1)} %copy.6.twiddle_ref, ...), custom_call_target="tpu_custom_call" | custom-call | tf_op jit(solution)/shard_map/dedisperse/pallas_call | solution.py:408
  (17 shorter events, 0.2 us)
Async XLA Ops:
  6.5 54.0 %all-to-all-start = ((bf16[16,256,256]{2,1,0:T(8,128)(2,1)}), bf16[16,256,256]{2,1,0:T(8,128)(2,1)S(1)}, u32[]{:S(2)}, u32[]{:S(2)}) async-start(bf16[16,256,256]{2,1,0:T(8,128)(2,1)} %form_beams.1), calls=%async_computation | async-start | bytes 4194304 | tf_op jit(solution)/shard_map/all_to_all | solution.py:432

commit v6 on v5

--- a/solution.py
+++ b/solution.py
@@ -105,7 +105,7 @@
     group_combs = group // part_rows
     groups = chan_dev // group
     chunks = volt_sem.shape[0]
-    ends = [groups * end // 16 for end in (6, 11, 14, 16)] if chunks > 1 else [groups]
+    ends = [groups * end // 16 for end in (5, 10, 14, 16)] if chunks > 1 else [groups]
     begins = [0] + ends[:-1]
 
     def volt_copy(g):
@@ -171,8 +171,9 @@
         if g in begins:
             chunk = begins.index(g)
             volt_copy(chunk).wait()
-            if chunk + 2 < chunks:
-                volt_copy(chunk + 2).start()
+            if chunk == 0:
+                for later in range(2, chunks):
+                    volt_copy(later).start()
         slot = g % rows_ref.shape[0]
         for i in range(0, group, 2):
             weights, sources = [], []
@@ -381,7 +382,7 @@
     tiles = samples // 8
     for half in range(2):
 
-        @pl.loop(0, tiles, unroll=1)
+        @pl.loop(0, tiles, unroll=2)
         def _(tile):
             spread(half * tiles + tile)
 

time: 68.7 us -> 68.4 us (level)
  no operation moved by 1% of the time
where the time goes in v6:
time: 68.4 us; the launch traced here: 68.2 us
  waiting for transfers between devices  41.4 us (61%)
  Pallas kernels  14.2 us (21%)
  starting transfers between devices  6.55 us (10%)
  other arithmetic  3.27 us (5%)
  between operations  2.03 us (3%)
  local copies, waits for them, and re-layouts  0.75 us (1%)
    all_to_all x1, waiting for transfers between devices, on_device(): lax.all_to_all(formed, 'chan', split_axis=0, concat_axis=0, tiled=True)  41.4 us
    pallas_call x1, Pallas kernels, dedisperse(): pl.pallas_call(functools.partial(dedisperse_kernel, chans), out_shape=jax...  7.88 us
    all_to_all x1, starting transfers between devices, on_device(): lax.all_to_all(formed, 'chan', split_axis=0, concat_axis=0, tiled=True)  6.55 us
    pallas_call x1, Pallas kernels, form_beams(): pl.pallas_call(functools.partial(beam_kernel, chans, comb), out_shape=jax...  6.32 us
    another operation x3, other arithmetic  2 us
  transfers between devices with their start and end apart: 1, of which 1 were waited for; matrix products, arithmetic and copies ran while one was open for 6% of the time, Pallas kernels for 0%

profile of v6, /device:TPU:13, one launch (start us, length us, event | category | flops | bytes accessed | tf_op | source)
XLA Modules:
  0.0 68.2 jit_solution(4446856659118017879)
XLA Ops:
  0.0 6.3 %form_beams.1 = bf16[16,256,256]{2,1,0:T(8,128)(2,1)} custom-call(s32[16]{0:T(128)} %point_ref.1, f32[64,512]{1,0:T(8,128)} %bitcast.15, s32[1,64]{1,0:T(1,128)} %bitcast.16, bf16[16,16,128,128]{3,2,1,0:T(8,128)(2,1)} %bitcast.14), custom_call_target="tpu_custom_call" | custom-call | tf_op jit(solution)/shard_map/form_beams/pallas_call | solution.py:217
  6.3 6.6 %all-to-all-start = ((bf16[16,256,256]{2,1,0:T(8,128)(2,1)}), bf16[16,256,256]{2,1,0:T(8,128)(2,1)S(1)}, u32[]{:S(2)}, u32[]{:S(2)}) async-start(bf16[16,256,256]{2,1,0:T(8,128)(2,1)} %form_beams.1), calls=%async_computation | async-start | bytes 4194304 | tf_op jit(solution)/shard_map/all_to_all | solution.py:433
  13.6 0.1 fusion.95
  13.6 0.1 maximum_reduce_fusion
  13.7 0.6 fusion.97
  15.6 0.1 fusion.65
  15.7 0.1 copy.6.twiddle_ref
  16.0 0.1 multiply_subtract_fusion
  16.1 0.1 fusion.76
  16.3 0.2 fusion.72
  16.4 0.3 fusion.31
  16.7 0.3 negate_convert_fusion
  17.1 0.4 fusion.29
  17.5 1.4 %cosine_convert_fusion = (bf16[32,1,8,256]{3,2,1,0:T(8,128)(2,1)S(1)}, bf16[32,1,8,256]{3,2,1,0:T(8,128)(2,1)S(1)}) fusion(s32[32,8]{1,0:T(8,128)S(1)} %multiply_add_fusion), kind=kLoop, calls=%fused_computation.14 | loop fusion | flops 1900544 | bytes 263168 | tf_op jit(solution)/shard_map/convert
  18.9 41.4 %all-to-all-done = bf16[16,256,256]{2,1,0:T(8,128)(2,1)S(1)} async-done(((bf16[16,256,256]{2,1,0:T(8,128)(2,1)}), bf16[16,256,256]{2,1,0:T(8,128)(2,1)S(1)}, u32[]{:S(2)}, u32[]{:S(2)}) %all-to-all-start) | async-done | bytes 2097184 | tf_op jit(solution)/shard_map/all_to_all | solution.py:433
  60.3 7.9 %dedisperse.1 = f32[1,2,128,4096]{3,2,1,0:T(8,128)} custom-call(s32[1]{0:T(128)S(6)} %copy.7.rate_ref, bf16[16,16,16,256]{3,2,1,0:T(8,128)(2,1)S(1)} %bitcast.12, bf16[256,256]{1,0:T(8,128)(2,1)S(1)} %maximum_maximum_fusion.time_ref, bf16[512,256]{1,0:T(8,128)(2,1)S(1)} %bitcast.13, f32[2,256,16]{2,1,0:T(8,128)S(1)} %copy.6.twiddle_ref, ...), custom_call_target="tpu_custom_call" | custom-call | tf_op jit(solution)/shard_map/dedisperse/pallas_call | solution.py:409
  (17 shorter events, 0.2 us)
Async XLA Ops:
  6.3 54.0 %all-to-all-start = ((bf16[16,256,256]{2,1,0:T(8,128)(2,1)}), bf16[16,256,256]{2,1,0:T(8,128)(2,1)S(1)}, u32[]{:S(2)}, u32[]{:S(2)}) async-start(bf16[16,256,256]{2,1,0:T(8,128)(2,1)} %form_beams.1), calls=%async_computation | async-start | bytes 4194304 | tf_op jit(solution)/shard_map/all_to_all | solution.py:433

commit v7 on v6

--- a/solution.py
+++ b/solution.py
@@ -325,20 +325,19 @@
     factor = lax.rsqrt(jnp.full((1, samples), mean_power, F32) + EPSILON)
     for p in range(2):
         scaled_ref[p] = after_ref[p] * factor
-    for c_b in range(comb):
-        moved = moved_ref[c_b]
-
+    for first in range(0, comb, 2):
+        moved = jnp.concatenate([moved_ref[first], moved_ref[first + 1]], 1)
         mixed = jnp.dot(mix_ref[...], moved, preferred_element_type=F32)
-        for i in range(low // 8):
-            rows = pl.ds(8 * i, 8)
-            by_re, by_im = mixed[16 * i : 16 * i + 8], mixed[16 * i + 8 : 16 * i + 16]
-            values = (
-                by_re[:, :samples] - by_im[:, samples:],
-                by_re[:, samples:] + by_im[:, :samples],
-            )
-            if c_b:
-                values = cmul(values, [twiddle_ref[p, rows, c_b : c_b + 1] for p in range(2)])
-            grid_ref[c_b, 0, rows], grid_ref[c_b, 1, rows] = values
+        for c_b in range(first, first + 2):
+            at = (c_b - first) * 2 * samples
+            mid, end = at + samples, at + 2 * samples
+            for i in range(low // 8):
+                rows = pl.ds(8 * i, 8)
+                by_re, by_im = mixed[16 * i : 16 * i + 8], mixed[16 * i + 8 : 16 * i + 16]
+                values = (by_re[:, at:mid] - by_im[:, mid:end], by_re[:, mid:end] + by_im[:, at:mid])
+                if c_b:
+                    values = cmul(values, [twiddle_ref[p, rows, c_b : c_b + 1] for p in range(2)])
+                grid_ref[c_b, 0, rows], grid_ref[c_b, 1, rows] = values
 
     rate = 2 * rate_ref[0] + 1
 

time: 68.4 us -> 68.4 us (level)
  no operation moved by 1% of the time
where the time goes in v7:
time: 68.4 us; the launch traced here: 68.2 us
  waiting for transfers between devices  41.4 us (61%)
  Pallas kernels  14.2 us (21%)
  starting transfers between devices  6.55 us (10%)
  other arithmetic  3.27 us (5%)
  between operations  2.03 us (3%)
  local copies, waits for them, and re-layouts  0.75 us (1%)
    all_to_all x1, waiting for transfers between devices, on_device(): lax.all_to_all(formed, 'chan', split_axis=0, concat_axis=0, tiled=True)  41.4 us
    pallas_call x1, Pallas kernels, dedisperse(): pl.pallas_call(functools.partial(dedisperse_kernel, chans), out_shape=jax...  7.87 us
    all_to_all x1, starting transfers between devices, on_device(): lax.all_to_all(formed, 'chan', split_axis=0, concat_axis=0, tiled=True)  6.55 us
    pallas_call x1, Pallas kernels, form_beams(): pl.pallas_call(functools.partial(beam_kernel, chans, comb), out_shape=jax...  6.32 us
    another operation x3, other arithmetic  2 us
  transfers between devices with their start and end apart: 1, of which 1 were waited for; matrix products, arithmetic and copies ran while one was open for 6% of the time, Pallas kernels for 0%

profile of v7, /device:TPU:13, one launch (start us, length us, event | category | flops | bytes accessed | tf_op | source)
XLA Modules:
  0.0 68.2 jit_solution(794444098255331155)
XLA Ops:
  0.0 6.3 %form_beams.1 = bf16[16,256,256]{2,1,0:T(8,128)(2,1)} custom-call(s32[16]{0:T(128)} %point_ref.1, f32[64,512]{1,0:T(8,128)} %bitcast.15, s32[1,64]{1,0:T(1,128)} %bitcast.16, bf16[16,16,128,128]{3,2,1,0:T(8,128)(2,1)} %bitcast.14), custom_call_target="tpu_custom_call" | custom-call | tf_op jit(solution)/shard_map/form_beams/pallas_call | solution.py:217
  6.3 6.6 %all-to-all-start = ((bf16[16,256,256]{2,1,0:T(8,128)(2,1)}), bf16[16,256,256]{2,1,0:T(8,128)(2,1)S(1)}, u32[]{:S(2)}, u32[]{:S(2)}) async-start(bf16[16,256,256]{2,1,0:T(8,128)(2,1)} %form_beams.1), calls=%async_computation | async-start | bytes 4194304 | tf_op jit(solution)/shard_map/all_to_all | solution.py:432
  13.6 0.1 fusion.95
  13.6 0.1 maximum_reduce_fusion
  13.7 0.6 fusion.97
  15.6 0.1 fusion.65
  15.7 0.1 copy.6.twiddle_ref
  16.0 0.1 multiply_subtract_fusion
  16.1 0.1 fusion.76
  16.3 0.2 fusion.72
  16.4 0.3 fusion.31
  16.7 0.3 negate_convert_fusion
  17.1 0.4 fusion.29
  17.5 1.4 %cosine_convert_fusion = (bf16[32,1,8,256]{3,2,1,0:T(8,128)(2,1)S(1)}, bf16[32,1,8,256]{3,2,1,0:T(8,128)(2,1)S(1)}) fusion(s32[32,8]{1,0:T(8,128)S(1)} %multiply_add_fusion), kind=kLoop, calls=%fused_computation.14 | loop fusion | flops 1900544 | bytes 263168 | tf_op jit(solution)/shard_map/convert
  18.9 41.4 %all-to-all-done = bf16[16,256,256]{2,1,0:T(8,128)(2,1)S(1)} async-done(((bf16[16,256,256]{2,1,0:T(8,128)(2,1)}), bf16[16,256,256]{2,1,0:T(8,128)(2,1)S(1)}, u32[]{:S(2)}, u32[]{:S(2)}) %all-to-all-start) | async-done | bytes 2097184 | tf_op jit(solution)/shard_map/all_to_all | solution.py:432
  60.3 7.9 %dedisperse.1 = f32[1,2,128,4096]{3,2,1,0:T(8,128)} custom-call(s32[1]{0:T(128)S(6)} %copy.7.rate_ref, bf16[16,16,16,256]{3,2,1,0:T(8,128)(2,1)S(1)} %bitcast.12, bf16[256,256]{1,0:T(8,128)(2,1)S(1)} %maximum_maximum_fusion.time_ref, bf16[512,256]{1,0:T(8,128)(2,1)S(1)} %bitcast.13, f32[2,256,16]{2,1,0:T(8,128)S(1)} %copy.6.twiddle_ref, ...), custom_call_target="tpu_custom_call" | custom-call | tf_op jit(solution)/shard_map/dedisperse/pallas_call | solution.py:408
  (17 shorter events, 0.2 us)
Async XLA Ops:
  6.3 54.0 %all-to-all-start = ((bf16[16,256,256]{2,1,0:T(8,128)(2,1)}), bf16[16,256,256]{2,1,0:T(8,128)(2,1)S(1)}, u32[]{:S(2)}, u32[]{:S(2)}) async-start(bf16[16,256,256]{2,1,0:T(8,128)(2,1)} %form_beams.1), calls=%async_computation | async-start | bytes 4194304 | tf_op jit(solution)/shard_map/all_to_all | solution.py:432
